TPU v7x, 32 devices: a whole 2x2x4 slice. The times are simulated.
32 devices in a mesh: groups: 2 (over x), dp: 8 (over z, y), tensor: 2 (over core).
Axes of the slice: x: 2, y: 2, z: 4, core: 2. Of those that a mesh axis runs over, the one named last changes fastest.
Arguments:
- tokens: bfloat16 [8192, 5120], P(('groups', 'dp'), 'tensor'), parts along dimension 0, may hold values from -6 to 6
- frozen_value_weight: bfloat16 [5120, 768], P('tensor'), may hold values from -0.078125 to 0.078125
- adapter_down_weight: bfloat16 [128, 16, 5120], P('dp', None, 'tensor'), may hold values from -0.078125 to 0.078125
- adapter_up_weight: bfloat16 [128, 16, 768], P('dp'), may hold values from -0.25 to 2
- segment_adapter_index: int32 [512], P(('groups', 'dp')), parts along dimension 0, may hold values from 0 to 127, as said below
- segment_live_length: int32 [512], P(('groups', 'dp')), parts along dimension 0, may hold values from 1 to 16
- cotangent: bfloat16 [8192, 768], P(('groups', 'dp')), parts along dimension 0, may hold values from -3 to 7.5
Outputs:
- output: bfloat16 [8192, 768], P(('groups', 'dp'), 'tensor'), parts along dimension 0
- input_gradient: bfloat16 [8192, 5120], P(('groups', 'dp'), 'tensor'), parts along dimension 0
- grad_down: bfloat16 [256, 16, 5120], P(('groups', 'dp'), None, 'tensor'), parts along dimension 0
- grad_up: bfloat16 [256, 16, 768], P(('groups', 'dp'), None, 'tensor'), parts along dimension 0
There are 2 independent parts, one for each index of `groups`. A program takes and returns all parts, laid end to end along the dimension named above; an argument that names none is the same for every part. Nothing has to cross between parts.
Inputs may be any that keep to these rules, and one draw needn't show every extreme that they name: `segment_adapter_index`: adapter b is owned by index b // 16 of dp. Among the 32 segments of one device (aligned blocks), at most 4 name adapters of any one owner, and on every device some owner is named by exactly 4 of them.
All inputs are finite; a program needn't handle non-finite values.
Results may differ from a plain program's by a relative error of at most 0.0052.
Values may be sent and summed in bfloat16 or wider, within the bound.
A program may use at most 128 MiB of HBM per device.

v0:
```python
import jax
import jax.numpy as jnp
from jax import lax
from jax.sharding import PartitionSpec as P

adapter_scale = 2.0


def select_rows(picker, rows):
    return lax.dot_general(
        picker, rows, (((0,), (0,)), ((), ())), preferred_element_type=jnp.float32
    )


def local(
    tokens,
    frozen_value_weight,
    adapter_down_weight,
    adapter_up_weight,
    segment_adapter_index,
    segment_live_length,
    cotangent,
):
    dp_count = lax.axis_size("dp")
    seg_dev = segment_adapter_index.shape[0]
    seg_len = tokens.shape[0] // seg_dev
    tok_rows = tokens.shape[0]
    half_d = tokens.shape[1]
    full_out = frozen_value_weight.shape[1]
    half_out = full_out // lax.axis_size("tensor")
    adapter_rank_width = adapter_down_weight.shape[1]
    segment_token_count = adapter_down_weight.shape[0]
    per_owner = max(1, -(-seg_dev // dp_count))
    n_slots = dp_count * per_owner
    column = lax.axis_index("tensor") * half_out
    owners_of = segment_adapter_index // segment_token_count
    local_index = segment_adapter_index - owners_of * segment_token_count
    positions = jnp.arange(seg_dev, dtype=jnp.int32)
    earlier = (owners_of[:, None] == owners_of[None, :]) & (positions[None, :] < positions[:, None])
    placed = owners_of * per_owner + jnp.sum(earlier.astype(jnp.int32), axis=1)
    picker = placed[None, :] == jnp.arange(n_slots, dtype=jnp.int32)[:, None]
    request = jnp.sum(jnp.where(picker, local_index[None, :] + 1, 0), axis=1).reshape(
        dp_count, per_owner
    )
    requested = lax.all_to_all(request, "dp", split_axis=0, concat_axis=0, tiled=True)
    chooser = (
        requested.reshape(n_slots, 1) - 1
        == jnp.arange(segment_token_count, dtype=jnp.int32)[None, :]
    )
    select_bfloat_path = chooser.astype(jnp.bfloat16)
    down_sent = jnp.dot(
        select_bfloat_path,
        adapter_down_weight.reshape(segment_token_count, -1),
        preferred_element_type=jnp.float32,
    ).astype(jnp.bfloat16)
    up_sent = jnp.dot(
        select_bfloat_path,
        adapter_up_weight.reshape(segment_token_count, -1),
        preferred_element_type=jnp.float32,
    ).astype(jnp.bfloat16)
    down_got, up_got = (
        lax.all_to_all(
            down_sent.reshape(dp_count, per_owner, -1),
            "dp",
            split_axis=0,
            concat_axis=0,
            tiled=True,
        ),
        lax.all_to_all(
            up_sent.reshape(dp_count, per_owner, -1), "dp", split_axis=0, concat_axis=0, tiled=True
        ),
    )
    pick_bf = picker.astype(jnp.bfloat16)
    segment_down_weight = (
        select_rows(pick_bf, down_got.reshape(n_slots, -1))
        .astype(jnp.bfloat16)
        .reshape(seg_dev, adapter_rank_width, half_d)
    )
    segment_up_weight = (
        select_rows(pick_bf, up_got.reshape(n_slots, -1))
        .astype(jnp.bfloat16)
        .reshape(seg_dev, adapter_rank_width, full_out)
    )
    token_seg = tokens.reshape(seg_dev, seg_len, half_d)
    slot_pos = jnp.arange(seg_len, dtype=jnp.int32)
    active_token_mask = (slot_pos[None, :] < segment_live_length[:, None]).astype(jnp.float32)[
        :, :, None
    ]
    shrunk_part = jnp.einsum(
        "std,srd->str", token_seg, segment_down_weight, preferred_element_type=jnp.float32
    )
    reduced_activations = (lax.psum(shrunk_part, "tensor") * active_token_mask).astype(jnp.bfloat16)
    base_part = jnp.dot(tokens, frozen_value_weight, preferred_element_type=jnp.float32)
    frozen_output_sum = lax.psum_scatter(base_part, "tensor", scatter_dimension=1, tiled=True)
    up_half = lax.dynamic_slice_in_dim(segment_up_weight, column, half_out, 2)
    expand_rank = jnp.einsum(
        "str,sro->sto", reduced_activations, up_half, preferred_element_type=jnp.float32
    ).reshape(tok_rows, half_out)
    output = (frozen_output_sum + adapter_scale * expand_rank).astype(jnp.bfloat16)
    segment_output_gradient = cotangent.reshape(seg_dev, seg_len, full_out)
    reduced_gradient = (
        adapter_scale
        * jnp.einsum(
            "wad,wzd->waz",
            segment_output_gradient,
            segment_up_weight,
            preferred_element_type=jnp.float32,
        )
        * active_token_mask
    ).astype(jnp.bfloat16)
    frozen_backward = lax.dot_general(
        cotangent, frozen_value_weight, (((1,), (1,)), ((), ())), preferred_element_type=jnp.float32
    )
    adapter_backward = jnp.einsum(
        "omg,ogv->omv", reduced_gradient, segment_down_weight, preferred_element_type=jnp.float32
    ).reshape(tok_rows, half_d)
    input_gradient = (frozen_backward + adapter_backward).astype(jnp.bfloat16)
    cotan_half = lax.dynamic_slice_in_dim(segment_output_gradient, column, half_out, 2)
    down_terms = jnp.einsum(
        "str,std->srd", reduced_gradient, token_seg, preferred_element_type=jnp.float32
    ).reshape(seg_dev, -1)
    up_projection_terms = (
        adapter_scale
        * jnp.einsum(
            "ubd,ubp->udp", reduced_activations, cotan_half, preferred_element_type=jnp.float32
        )
    ).reshape(seg_dev, -1)
    seg_of_slot = jnp.sum(jnp.where(picker, positions[None, :], 0), axis=1)
    occupied = jnp.any(picker, axis=1)[:, None]
    down_send = jnp.where(occupied, jnp.take(down_terms, seg_of_slot, axis=0), 0.0)
    up_send = jnp.where(occupied, jnp.take(up_projection_terms, seg_of_slot, axis=0), 0.0)
    got_down, got_up = (
        lax.all_to_all(
            down_send.reshape(dp_count, per_owner, -1),
            "dp",
            split_axis=0,
            concat_axis=0,
            tiled=True,
        ),
        lax.all_to_all(
            up_send.reshape(dp_count, per_owner, -1), "dp", split_axis=0, concat_axis=0, tiled=True
        ),
    )
    choose_f = chooser.astype(jnp.float32)
    grad_down = lax.dot_general(
        choose_f,
        got_down.reshape(n_slots, -1),
        (((0,), (0,)), ((), ())),
        precision=lax.Precision.HIGHEST,
    )
    grad_up = lax.dot_general(
        choose_f,
        got_up.reshape(n_slots, -1),
        (((0,), (0,)), ((), ())),
        precision=lax.Precision.HIGHEST,
    )
    grad_down = grad_down.reshape(segment_token_count, adapter_rank_width, half_d).astype(
        jnp.bfloat16
    )
    grad_up = grad_up.reshape(segment_token_count, adapter_rank_width, half_out).astype(
        jnp.bfloat16
    )
    return (output, input_gradient, grad_down, grad_up)


def solution(mesh):
    in_specs = (
        P(("groups", "dp"), "tensor"),
        P("tensor", None),
        P("dp", None, "tensor"),
        P("dp", None, None),
        P(("groups", "dp")),
        P(("groups", "dp")),
        P(("groups", "dp"), None),
    )
    out_specs = (
        P(("groups", "dp"), "tensor"),
        P(("groups", "dp"), "tensor"),
        P(("groups", "dp"), None, "tensor"),
        P(("groups", "dp"), None, "tensor"),
    )
    return jax.shard_map(local, mesh=mesh, in_specs=in_specs, out_specs=out_specs, check_vma=False)
```

profile of v0, /device:TPU:0, one launch (start us, length us, event | category | flops | bytes accessed | tf_op | source)
XLA Modules:
  0.0 296.7 jit_solution(160717908440968503)
XLA Ops:
  7.2 0.8 subtract_add_fusion
  8.0 0.2 convert_reduce_fusion
  8.2 0.1 select_reduce_fusion
  8.3 0.7 all_to_all.18
  9.0 7.3 %all-to-all-start = ((s32[8,1,4]{2,1,0:T(1,128)}), s32[8,1,4]{2,1,0:T(1,128)S(1)}, u32[]{:S(2)}, u32[]{:S(2)}) async-start(s32[8,1,4]{2,1,0:T(1,128)} %bitcast), calls=%async_computation.1 | async-start | bytes 8192 | tf_op jit(solution)/shard_map/all_to_all | solution.py:45
  16.3 1.9 copy.41
  18.1 4.5 %all-to-all-done = s32[8,1,4]{2,1,0:T(1,128)S(1)} async-done(((s32[8,1,4]{2,1,0:T(1,128)}), s32[8,1,4]{2,1,0:T(1,128)S(1)}, u32[]{:S(2)}, u32[]{:S(2)}) %all-to-all-start) | async-done | bytes 160 | tf_op jit(solution)/shard_map/all_to_all | solution.py:45
  22.7 0.1 sub.18
  22.8 1.4 convolution_convert_fusion.3
  24.2 1.2 reshape.149
  25.3 3.5 %all-to-all-start.2 = ((bf16[8,4,12288]{2,1,0:T(4,128)(2,1)}), bf16[8,4,12288]{2,1,0:T(4,128)(2,1)S(1)}, u32[]{:S(2)}, u32[]{:S(2)}) async-start(bf16[8,4,12288]{2,1,0:T(4,128)(2,1)} %reshape.149), calls=%async_computation.3 | async-start | bytes 1572864 | tf_op jit(solution)/shard_map/all_to_all | solution.py:69
  28.9 2.0 copy.39
  30.9 2.4 convolution_convert_fusion.1
  33.3 4.4 %reshape.144 = bf16[8,4,40960]{2,1,0:T(4,128)(2,1)} reshape(bf16[32,40960]{1,0:T(8,128)(2,1)} %convolution_convert_fusion.1) | data formatting | bytes 5242880 | tf_op jit(solution)/shard_map/reshape | solution.py:63
  37.7 10.2 %all-to-all-done.2 = bf16[8,4,12288]{2,1,0:T(4,128)(2,1)S(1)} async-done(((bf16[8,4,12288]{2,1,0:T(4,128)(2,1)}), bf16[8,4,12288]{2,1,0:T(4,128)(2,1)S(1)}, u32[]{:S(2)}, u32[]{:S(2)}) %all-to-all-start.2) | async-done | bytes 786464 | tf_op jit(solution)/shard_map/all_to_all | solution.py:69
  47.9 4.6 %all-to-all-start.1 = ((bf16[8,4,40960]{2,1,0:T(4,128)(2,1)}), bf16[8,4,40960]{2,1,0:T(4,128)(2,1)}, u32[]{:S(2)}, u32[]{:S(2)}) async-start(bf16[8,4,40960]{2,1,0:T(4,128)(2,1)} %reshape.144), calls=%async_computation.2 | async-start | bytes 5242880 | tf_op jit(solution)/shard_map/all_to_all | solution.py:62
  52.5 0.1 fusion.15
  52.6 0.6 broadcast_in_dim.77
  53.3 0.1 reduce_sum.34
  53.3 0.6 pad_clamp_fusion
  53.9 0.5 compare_and_fusion
  54.5 0.1 fusion.14
  54.6 0.7 fusion.13
  55.2 1.1 reshape.150
  56.3 1.6 convolution_convert_fusion.2
  57.9 0.1 copy.42
  58.1 0.4 fusion.7
  58.5 0.5 copy-done.2
  59.0 0.8 fusion.31
  59.8 5.4 %copy.43 = f32[4,8,16,2560]{3,1,2,0:T(8,128)} copy(f32[4,8,16,2560]{3,2,1,0:T(8,128)S(1)} %bitcast.68) | data formatting | bytes 10485760
  65.2 9.1 %gather_fusion = f32[32,40960]{1,0:T(8,128)} fusion(f32[32,40960]{1,0:T(8,128)} %bitcast.63, s32[1024]{0:T(1024)} %pad_clamp_fusion), kind=kCustom, calls=%fused_computation | custom fusion | bytes 10485888 | tf_op jit(solution)/shard_map/jit(_take)/gather | solution.py:130
  74.2 5.9 %gather.13 = f32[8,4,40960]{2,1,0:T(4,128)} reshape(f32[32,40960]{1,0:T(8,128)} %gather_fusion) | data formatting | bytes 10485760 | tf_op jit(solution)/shard_map/jit(_take)/gather | solution.py:130
  80.1 30.7 %all-to-all-done.1 = bf16[8,4,40960]{2,1,0:T(4,128)(2,1)} async-done(((bf16[8,4,40960]{2,1,0:T(4,128)(2,1)}), bf16[8,4,40960]{2,1,0:T(4,128)(2,1)}, u32[]{:S(2)}, u32[]{:S(2)}) %all-to-all-start.1) | async-done | bytes 2621472 | tf_op jit(solution)/shard_map/all_to_all | solution.py:62
  110.9 4.2 %reshape.145 = bf16[32,40960]{1,0:T(8,128)(2,1)} reshape(bf16[8,4,40960]{2,1,0:T(4,128)(2,1)} %all-to-all-done.1) | data formatting | bytes 5242880 | tf_op jit(solution)/shard_map/reshape | solution.py:75
  115.1 2.6 convolution_convert_fusion
  117.7 0.8 copy.40
  118.5 1.5 copy-done.1
  120.0 1.2 convolution_bitcast_fusion
  121.2 4.2 %psum.7 = f32[32,16,16]{1,2,0:T(8,128)S(1)} all-reduce(f32[32,16,16]{1,2,0:T(8,128)S(1)} %convolution_bitcast_fusion), channel_id=1, replica_groups=mesh['groups'=2,'dp'=8,'tensor'=2] {'tensor'}, use_global_device_ids=true, to_apply=%region_3.4 | all-reduce | flops 8192 | bytes 65536 | tf_op jit(solution)/shard_map/psum | solution.py:92
  125.5 1.4 convolution_multiply_fusion
  126.8 0.2 copy.44
  127.1 1.8 gather_fusion.1
  128.9 1.4 gather.15
  130.2 1.8 select_select_fusion.1
  132.0 3.6 %all-to-all-start.4 = ((f32[8,4,6144]{2,1,0:T(4,128)}), f32[8,4,6144]{2,1,0:T(4,128)S(1)}, u32[]{:S(2)}, u32[]{:S(2)}) async-start(f32[8,4,6144]{2,1,0:T(4,128)} %select_select_fusion.1), calls=%async_computation.5 | async-start | bytes 1572864 | tf_op jit(solution)/shard_map/all_to_all | solution.py:140
  135.6 6.2 %select_select_fusion = f32[8,4,40960]{2,1,0:T(4,128)} fusion(f32[8,4,40960]{2,1,0:T(4,128)} %gather.13, pred[8,4]{1,0:T(8,128)(4,1)} %compare_and_fusion, pred[8,4]{1,0:T(8,128)(4,1)} %broadcast_in_dim.77), kind=kLoop, calls=%fused_computation.11 | loop fusion | flops 2621440 | bytes 10485824 | tf_op jit(solution)/shard_map/jit(_where)/select_n | solution.py:130
  141.8 14.6 %all-to-all-done.4 = f32[8,4,6144]{2,1,0:T(4,128)S(1)} async-done(((f32[8,4,6144]{2,1,0:T(4,128)}), f32[8,4,6144]{2,1,0:T(4,128)S(1)}, u32[]{:S(2)}, u32[]{:S(2)}) %all-to-all-start.4) | async-done | bytes 786464 | tf_op jit(solution)/shard_map/all_to_all | solution.py:140
  156.4 0.9 copy-done.4
  157.3 4.7 %all-to-all-start.3 = ((f32[8,4,40960]{2,1,0:T(4,128)}), f32[8,4,40960]{2,1,0:T(4,128)}, u32[]{:S(2)}, u32[]{:S(2)}) async-start(f32[8,4,40960]{2,1,0:T(4,128)} %select_select_fusion), calls=%async_computation.4 | async-start | bytes 10485760 | tf_op jit(solution)/shard_map/all_to_all | solution.py:133
  162.0 0.0 reduce-scatter.2.cloned.1.call-start
  162.0 5.5 %fusion.29 = f32[512,768]{1,0:T(8,128)} fusion(bf16[512,2560]{1,0:T(8,128)(2,1)S(1)} %copy-done, bf16[2560,768]{1,0:T(8,128)(2,1)} %param.8), kind=kOutput, calls=%fused_computation.59 | convolution fusion | flops 2013265920 | bytes 8126464 | tf_op jit(solution)/shard_map/dot_general | solution.py:93
  167.6 2.2 convolution_multiply_fusion.1
  169.7 8.3 %reduce-scatter.2.cloned.1.call-done = f32[512,384]{1,0:T(8,128)} async-done(((f32[512,768]{1,0:T(8,128)}), f32[512,384]{1,0:T(8,128)}) %reduce-scatter.2.cloned.1.call-update) | async-done | bytes 786448 | tf_op jit(solution)/shard_map/reduce_scatter | solution.py:94
  178.1 2.2 fusion.10
  180.3 2.8 fusion.30
  183.1 0.4 copy-done.15
  183.4 3.7 %fusion.3 = bf16[512,2560]{1,0:T(8,128)(2,1)} fusion(f32[32,16,2560]{2,1,0:T(8,128)S(1)} %fusion.30, bf16[512,768]{1,0:T(8,128)(2,1)S(1)} %copy-done.8, bf16[2560,768]{1,0:T(8,128)(2,1)S(1)} %copy-done.15), kind=kOutput, calls=%fused_computation.10 | convolution fusion | flops 2015887360 | bytes 12582912 | tf_op jit(solution)/shard_map/dot_general | solution.py:111
  187.1 1.1 reshape.157
  188.3 1.5 convolution_convert_fusion.4
  189.8 0.7 copy.34
  190.5 87.0 %all-to-all-done.3 = f32[8,4,40960]{2,1,0:T(4,128)} async-done(((f32[8,4,40960]{2,1,0:T(4,128)}), f32[8,4,40960]{2,1,0:T(4,128)}, u32[]{:S(2)}, u32[]{:S(2)}) %all-to-all-start.3) | async-done | bytes 5242912 | tf_op jit(solution)/shard_map/all_to_all | solution.py:133
  277.5 6.0 %reshape.155 = f32[32,40960]{1,0:T(8,128)} reshape(f32[8,4,40960]{2,1,0:T(4,128)} %all-to-all-done.3) | data formatting | bytes 10485760 | tf_op jit(solution)/shard_map/reshape | solution.py:147
  283.5 4.5 %fusion.4 = bf16[16,16,2560]{2,0,1:T(8,128)(2,1)S(1)} fusion(f32[4,16,8,2560]{3,2,1,0:T(8,128)} %bitcast.67, s32[32]{0:T(128)S(1)} %copy-done.11), kind=kOutput, calls=%fused_computation.12 | convolution fusion | flops 252314112 | bytes 6553728 | tf_op jit(solution)/shard_map/dot_general | solution.py:145
  288.0 1.8 copy.33
  (32 shorter events, 0.1 us)
Async XLA Ops:
  7.2 51.8 %copy-start = (bf16[512,2560]{1,0:T(8,128)(2,1)S(1)}, bf16[512,2560]{1,0:T(8,128)(2,1)}, u32[]{:S(2)}) copy-start(bf16[512,2560]{1,0:T(8,128)(2,1)} %param.7) | copy-start | bytes 7864324
  8.2 48.1 %copy-start.12 = (s32[32]{0:T(128)}, s32[32]{0:T(128)S(1)}, u32[]{:S(2)}) copy-start(s32[32]{0:T(128)S(1)} %multiply_add_fusion) | copy-start | bytes 388
  9.0 13.7 %all-to-all-start = ((s32[8,1,4]{2,1,0:T(1,128)}), s32[8,1,4]{2,1,0:T(1,128)S(1)}, u32[]{:S(2)}, u32[]{:S(2)}) async-start(s32[8,1,4]{2,1,0:T(1,128)} %bitcast), calls=%async_computation.1 | async-start | bytes 8192 | tf_op jit(solution)/shard_map/all_to_all | solution.py:45
  22.8 8.2 %copy-start.10 = (s32[32]{0:T(128)}, s32[32]{0:T(128)S(1)}, u32[]{:S(2)}) copy-start(s32[32]{0:T(128)S(1)} %sub.18) | copy-start | bytes 388
  25.3 22.6 %all-to-all-start.2 = ((bf16[8,4,12288]{2,1,0:T(4,128)(2,1)}), bf16[8,4,12288]{2,1,0:T(4,128)(2,1)S(1)}, u32[]{:S(2)}, u32[]{:S(2)}) async-start(bf16[8,4,12288]{2,1,0:T(4,128)(2,1)} %reshape.149), calls=%async_computation.3 | async-start | bytes 1572864 | tf_op jit(solution)/shard_map/all_to_all | solution.py:69
  37.7 16.8 %copy-start.14 = (s32[32]{0:T(128)S(1)}, s32[32]{0:T(128)}, u32[]{:S(2)}) copy-start(s32[32]{0:T(128)} %param.12) | copy-start | bytes 388
  47.9 63.0 %all-to-all-start.1 = ((bf16[8,4,40960]{2,1,0:T(4,128)(2,1)}), bf16[8,4,40960]{2,1,0:T(4,128)(2,1)}, u32[]{:S(2)}, u32[]{:S(2)}) async-start(bf16[8,4,40960]{2,1,0:T(4,128)(2,1)} %reshape.144), calls=%async_computation.2 | async-start | bytes 5242880 | tf_op jit(solution)/shard_map/all_to_all | solution.py:62
  56.3 1.8 copy-start.7
  56.3 1.8 copy-start.9
  58.1 0.9 copy-start.2
  80.1 35.0 %copy-start.13 = (s32[32]{0:T(128)S(1)}, s32[32]{0:T(128)}, u32[]{:S(2)}) copy-start(s32[32]{0:T(128)} %copy-done.12) | copy-start | bytes 388
  118.5 1.5 copy-start.1
  125.4 1.4 copy-start.6
  132.0 24.4 %all-to-all-start.4 = ((f32[8,4,6144]{2,1,0:T(4,128)}), f32[8,4,6144]{2,1,0:T(4,128)S(1)}, u32[]{:S(2)}, u32[]{:S(2)}) async-start(f32[8,4,6144]{2,1,0:T(4,128)} %select_select_fusion.1), calls=%async_computation.5 | async-start | bytes 1572864 | tf_op jit(solution)/shard_map/all_to_all | solution.py:140
  156.4 0.9 copy-start.4
  157.3 120.2 %all-to-all-start.3 = ((f32[8,4,40960]{2,1,0:T(4,128)}), f32[8,4,40960]{2,1,0:T(4,128)}, u32[]{:S(2)}, u32[]{:S(2)}) async-start(f32[8,4,40960]{2,1,0:T(4,128)} %select_select_fusion), calls=%async_computation.4 | async-start | bytes 10485760 | tf_op jit(solution)/shard_map/all_to_all | solution.py:133
  162.0 5.6 %copy-start.3 = (bf16[4,8,16,768]{3,2,1,0:T(8,128)(2,1)S(1)}, bf16[4,8,16,768]{3,2,1,0:T(8,128)(2,1)}, u32[]{:S(2)}) copy-start(bf16[4,8,16,768]{3,2,1,0:T(8,128)(2,1)} %copy-done.2) | copy-start | bytes 2359300
  162.0 16.1 %reduce-scatter.2.cloned.1.call-start = ((), (), s32[]{:S(2)}) async-start(), calls=%async_computation.6 | async-start | bytes 2359296 | tf_op jit(solution)/shard_map/reduce_scatter | solution.py:94
  180.3 2.8 copy-start.8
  180.3 3.1 %copy-start.15 = (bf16[2560,768]{1,0:T(8,128)(2,1)S(1)}, bf16[2560,768]{1,0:T(8,128)(2,1)}, u32[]{:S(2)}) copy-start(bf16[2560,768]{1,0:T(8,128)(2,1)} %param.8) | copy-start | bytes 11796484
  183.4 3.7 %copy-start.5 = (f32[8,4,6144]{2,1,0:T(4,128)S(1)}, f32[8,4,6144]{2,1,0:T(4,128)}, u32[]{:S(2)}) copy-start(f32[8,4,6144]{2,1,0:T(4,128)} %copy-done.4) | copy-start | bytes 2359300
  183.4 4.9 %copy-start.11 = (s32[32]{0:T(128)S(1)}, s32[32]{0:T(128)}, u32[]{:S(2)}) copy-start(s32[32]{0:T(128)} %copy-done.10) | copy-start | bytes 388
Sparse Core Ops, SparseCore 0:
  167.7 10.3 reduce-scatter.1
where the time goes:
time: 298 us; the launch traced here: 297 us
  waiting for transfers between devices  155 us (52%)
  local copies, waits for them, and re-layouts  53.8 us (18%)
  matrix products  31.9 us (11%)
  starting transfers between devices  23.7 us (8%)
  between operations  14.3 us (5%)
  other arithmetic  13.3 us (4%)
  blocking collectives  4.24 us (1%)
    all_to_all x1, waiting for transfers between devices, local(): lax.all_to_all(down_send.reshape(dp_count, per_owner, -1), 'dp', split_ax...  87 us
    all_to_all x1, waiting for transfers between devices, local(): lax.all_to_all(down_sent.reshape(dp_count, per_owner, -1), 'dp', split_ax...  30.7 us
    unnamed x40, local copies, waits for them, and re-layouts  16.2 us
    gather x2, local copies, waits for them, and re-layouts, local(): jnp.take(down_terms, seg_of_slot, axis=0)  15 us
    all_to_all x1, waiting for transfers between devices, local(): lax.all_to_all(up_send.reshape(dp_count, per_owner, -1), 'dp', split_axis...  14.6 us
    all_to_all x1, waiting for transfers between devices, local(): lax.all_to_all(up_sent.reshape(dp_count, per_owner, -1), 'dp', split_axis...  10.2 us
    reduce_scatter x1, waiting for transfers between devices, local(): lax.psum_scatter(base_part, 'tensor', scatter_dimension=1, tiled=True)  8.34 us
    all_to_all x1, starting transfers between devices, local(): lax.all_to_all(request, 'dp', split_axis=0, concat_axis=0, tiled=True)  7.28 us
  transfers between devices with their start and end apart: 6, of which 6 were waited for; matrix products, arithmetic and copies ran while one was open for 21% of the time, Pallas kernels for 0%

commit v1 on v0

v1 whole, which is shorter than its diff:
```python
import jax
import jax.numpy as jnp
from jax import lax
from jax.sharding import PartitionSpec as P

adapter_scale = 2.0
BF = jnp.bfloat16
F32 = jnp.float32


def mm(a, b, ca=1, cb=0, **kw):
    return lax.dot_general(
        a, b, (((ca,), (cb,)), ((), ())), preferred_element_type=F32, **kw
    )


def local(tokens, weight, down, up, index, length, cot):
    dp = lax.axis_size("dp")
    seg_dev = index.shape[0]
    rows, half_d = tokens.shape
    seg_len = rows // seg_dev
    full_out = weight.shape[1]
    half_out = full_out // lax.axis_size("tensor")
    n_own, rank = down.shape[0], down.shape[1]
    per_owner = max(1, -(-seg_dev // dp))
    n_slots = dp * per_owner
    n_tok, n_rank, n_ad = n_slots * seg_len, n_slots * rank, n_own * rank
    column = lax.axis_index("tensor") * half_out

    owners = index // n_own
    local_index = index - owners * n_own
    pos = jnp.arange(seg_dev, dtype=jnp.int32)
    earlier = (owners[:, None] == owners[None, :]) & (pos[None, :] < pos[:, None])
    placed = owners * per_owner + jnp.sum(earlier.astype(jnp.int32), axis=1)
    picker = placed[None, :] == jnp.arange(n_slots, dtype=jnp.int32)[:, None]
    request = jnp.sum(jnp.where(picker, local_index[None, :] + 1, 0), axis=1)
    requested = (
        lax.all_to_all(
            request.reshape(dp, per_owner), "dp", split_axis=0, concat_axis=0, tiled=True
        ).reshape(n_slots)
        - 1
    )

    row_i = jnp.arange(rows, dtype=jnp.int32)
    placed_row = jnp.repeat(placed, seg_len)
    dest = placed_row * seg_len + row_i % seg_len
    live = (row_i % seg_len < jnp.repeat(length, seg_len)).astype(F32)[:, None]
    tok_i = jnp.arange(n_tok, dtype=jnp.int32)
    rank_i = jnp.arange(n_rank, dtype=jnp.int32)
    ad_i = jnp.arange(n_ad, dtype=jnp.int32)
    r_i = jnp.arange(rank, dtype=jnp.int32)
    place = (tok_i[:, None] == dest[None, :]).astype(BF)
    source = jnp.repeat(requested, rank) * rank + rank_i % rank
    choose = (source[:, None] == ad_i[None, :]).astype(BF)
    own_block = placed_row[:, None] == (rank_i // rank)[None, :]
    ad_block = jnp.repeat(requested, seg_len)[:, None] == (ad_i // rank)[None, :]
    spread = (rank_i[None, :] % rank == r_i[:, None]).astype(BF)
    spread_ad = (ad_i[None, :] % rank == r_i[:, None]).astype(BF)

    def exchange(x):
        y = lax.all_to_all(
            x.reshape(dp, x.shape[0] // dp, x.shape[1]),
            "dp", split_axis=0, concat_axis=0, tiled=True,
        )
        return y.reshape(x.shape)

    cot_half = lax.dynamic_slice_in_dim(cot, column, half_out, 1)
    up2 = lax.dynamic_slice_in_dim(up.reshape(n_ad, full_out), column, half_out, 1)
    tok_got = exchange(mm(place, tokens).astype(BF))
    cot_got = exchange(mm(place, cot_half).astype(BF))
    up_got = exchange(mm(choose, up2).astype(BF))
    down_got = exchange(mm(choose, down.reshape(n_ad, half_d)).astype(BF))

    base = lax.psum_scatter(mm(tokens, weight), "tensor", scatter_dimension=1, tiled=True)

    def compact(full):
        masked = jnp.where(own_block, full, 0.0)
        return mm(masked, spread.astype(F32), 1, 1, precision=lax.Precision.HIGHEST)

    parts = jnp.concatenate(
        [compact(mm(tokens, down_got, 1, 1)), compact(mm(cot_half, up_got, 1, 1))], axis=1
    )
    sums = lax.psum(parts, "tensor") * live
    shrunk = sums[:, :rank].astype(BF)
    d_shrunk = (adapter_scale * sums[:, rank:]).astype(BF)
    both = jnp.concatenate([shrunk, d_shrunk], axis=1)
    both_got = exchange(mm(place, both).astype(BF))

    shrunk_wide = jnp.where(own_block, mm(shrunk, spread), 0.0).astype(BF)
    d_wide = jnp.where(own_block, mm(d_shrunk, spread), 0.0).astype(BF)
    output = (base + adapter_scale * mm(shrunk_wide, up_got)).astype(BF)
    input_gradient = (mm(cot, weight, 1, 1) + mm(d_wide, down_got)).astype(BF)

    s_ad = jnp.where(ad_block, mm(both_got[:, :rank], spread_ad), 0.0).astype(BF)
    d_ad = jnp.where(ad_block, mm(both_got[:, rank:], spread_ad), 0.0).astype(BF)
    grad_down = mm(d_ad, tok_got, 0, 0).astype(BF).reshape(n_own, rank, half_d)
    grad_up = (adapter_scale * mm(s_ad, cot_got, 0, 0)).astype(BF)
    return output, input_gradient, grad_down, grad_up.reshape(n_own, rank, half_out)


def solution(mesh):
    in_specs = (
        P(("groups", "dp"), "tensor"),
        P("tensor", None),
        P("dp", None, "tensor"),
        P("dp", None, None),
        P(("groups", "dp")),
        P(("groups", "dp")),
        P(("groups", "dp"), None),
    )
    out_specs = (
        P(("groups", "dp"), "tensor"),
        P(("groups", "dp"), "tensor"),
        P(("groups", "dp"), None, "tensor"),
        P(("groups", "dp"), None, "tensor"),
    )
    return jax.shard_map(local, mesh=mesh, in_specs=in_specs, out_specs=out_specs, check_vma=False)
```

time: 298 us -> 201 us (0.67)
  local copies, waits for them, and re-layouts: 53.8 us -> 2.35 us
  waiting for transfers between devices: 155 us -> 110 us
  matrix products: 31.9 us -> 43.8 us
  other arithmetic: 13.3 us -> 2.65 us
  blocking collectives: 4.24 us -> 0 us
  starting transfers between devices: 23.7 us -> 26.9 us
    all_to_all x5 -> x6, waiting for transfers between devices: 147 us -> 106 us  [the longest x5 99.7 us: exchange(): lax.all_to_all(x.reshape(dp, x.shape[0] // dp, x.shape[1]), 'dp', split_a...]
    gather x4 -> x0, local copies, waits for them, and re-layouts: 18.1 us -> none  [the longest x2 15 us: local(): jnp.take(down_terms, seg_of_slot, axis=0)]
    reshape x6 -> x5, local copies, waits for them, and re-layouts: 18 us -> 0.4 us  [the longest x2 0.12 us: exchange(): x.reshape(dp, x.shape[0] // dp, x.shape[1])]
    unnamed x40 -> x6, local copies, waits for them, and re-layouts: 16.2 us -> 0.85 us
    dot_general x14 -> x15, matrix products: 31.9 us -> 43.8 us  [mm(): lax.dot_general(a, b, (((ca,), (cb,)), ((), ())), preferred_element_type=...]
    reduce_scatter x1, waiting for transfers between devices: 8.34 us -> 0.01 us  [local(): lax.psum_scatter(mm(tokens, weight), 'tensor', scatter_dimension=1, tiled...]
    select_n x3 -> x2, other arithmetic: 8.01 us -> 0.01 us  [the longest x1 0.01 us: local(): source = jnp.repeat(requested, rank) * rank + rank_i % rank]
    psum x0 -> x1, waiting for transfers between devices: none -> 4.3 us  [local(): sums = lax.psum(parts, 'tensor') * live]
  transfers between devices with their start and end apart: 6 -> 8, of which waited for: 6 -> 6; matrix products, arithmetic and copies ran while one was open for 21% -> 22% of each run, Pallas kernels for 0% -> 0%
where the time goes in v1:
time: 201 us; the launch traced here: 200 us
  waiting for transfers between devices  110 us (55%)
  matrix products  43.8 us (22%)
  starting transfers between devices  26.9 us (13%)
  between operations  14.2 us (7%)
  other arithmetic  2.65 us (1%)
  local copies, waits for them, and re-layouts  2.35 us (1%)
    all_to_all x5, waiting for transfers between devices, exchange(): lax.all_to_all(x.reshape(dp, x.shape[0] // dp, x.shape[1]), 'dp', split_a...  99.7 us
    dot_general x15, matrix products, mm(): lax.dot_general(a, b, (((ca,), (cb,)), ((), ())), preferred_element_type=...  43.8 us
    all_to_all x5, starting transfers between devices, exchange(): lax.all_to_all(x.reshape(dp, x.shape[0] // dp, x.shape[1]), 'dp', split_a...  19.5 us
    all_to_all x1, starting transfers between devices, local(): lax.all_to_all(request.reshape(dp, per_owner), 'dp', split_axis=0, concat...  7.28 us
    all_to_all x1, waiting for transfers between devices, local(): lax.all_to_all(request.reshape(dp, per_owner), 'dp', split_axis=0, concat...  6.39 us
    psum x1, waiting for transfers between devices, local(): sums = lax.psum(parts, 'tensor') * live  4.3 us
  transfers between devices with their start and end apart: 8, of which 6 were waited for; matrix products, arithmetic and copies ran while one was open for 22% of the time, Pallas kernels for 0%

profile of v1, /device:TPU:0, one launch (start us, length us, event | category | flops | bytes accessed | tf_op | source)
XLA Modules:
  0.0 200.3 jit_solution(16832963075663626301)
XLA Ops:
  7.2 0.0 copy-start
  7.2 0.8 subtract_add_fusion
  8.0 0.2 convert_reduce_fusion
  8.2 0.1 select_reduce_fusion
  8.3 0.7 all_to_all.21
  9.0 7.3 %all-to-all-start = ((s32[8,1,4]{2,1,0:T(1,128)}), s32[8,1,4]{2,1,0:T(1,128)S(1)}, u32[]{:S(2)}, u32[]{:S(2)}) async-start(s32[8,1,4]{2,1,0:T(1,128)} %bitcast), calls=%async_computation.1 | async-start | bytes 8192 | tf_op jit(solution)/shard_map/all_to_all | solution.py:38
  16.3 6.4 %all-to-all-done = s32[8,1,4]{2,1,0:T(1,128)S(1)} async-done(((s32[8,1,4]{2,1,0:T(1,128)}), s32[8,1,4]{2,1,0:T(1,128)S(1)}, u32[]{:S(2)}, u32[]{:S(2)}) %all-to-all-start) | async-done | bytes 160 | tf_op jit(solution)/shard_map/all_to_all | solution.py:38
  22.7 0.1 sub.31
  22.8 0.1 broadcast_in_dim.32
  22.8 0.1 reshape.159
  22.9 2.0 %convolution_convert_fusion.3 = bf16[512,384]{1,0:T(8,128)(2,1)} fusion(s32[512]{0:T(512)S(1)} %multiply_add_fusion.1, bf16[256,768]{1,0:T(8,128)(2,1)} %bitcast.49, s32[]{:T(128)S(6)} %select_n.111), kind=kOutput, calls=%fused_computation.14 | convolution fusion | flops 100990976 | bytes 591876 | tf_op jit(solution)/shard_map/dot_general | solution.py:12
  24.9 3.5 %all-to-all-start.2 = ((bf16[8,64,384]{2,1,0:T(8,128)(2,1)}), bf16[8,64,384]{2,1,0:T(8,128)(2,1)S(1)}, u32[]{:S(2)}, u32[]{:S(2)}) async-start(bf16[8,64,384]{2,1,0:T(8,128)(2,1)} %bitcast.6), calls=%async_computation.3 | async-start | bytes 786432 | tf_op jit(solution)/shard_map/all_to_all | solution.py:61
  28.4 3.7 %convolution_convert_fusion.1 = bf16[512,2560]{1,0:T(8,128)(2,1)} fusion(bf16[256,2560]{1,0:T(8,128)(2,1)} %bitcast.45, s32[512]{0:T(512)S(1)} %multiply_add_fusion.1), kind=kOutput, calls=%fused_computation.2 | convolution fusion | flops 672530432 | bytes 3934208 | tf_op jit(solution)/shard_map/dot_general | solution.py:12
  32.1 6.8 %all-to-all-done.2 = bf16[8,64,384]{2,1,0:T(8,128)(2,1)S(1)} async-done(((bf16[8,64,384]{2,1,0:T(8,128)(2,1)}), bf16[8,64,384]{2,1,0:T(8,128)(2,1)S(1)}, u32[]{:S(2)}, u32[]{:S(2)}) %all-to-all-start.2) | async-done | bytes 393248 | tf_op jit(solution)/shard_map/all_to_all | solution.py:61
  38.9 4.4 %all-to-all-start.1 = ((bf16[8,64,2560]{2,1,0:T(8,128)(2,1)}), bf16[8,64,2560]{2,1,0:T(8,128)(2,1)}, u32[]{:S(2)}, u32[]{:S(2)}) async-start(bf16[8,64,2560]{2,1,0:T(8,128)(2,1)} %bitcast.41), calls=%async_computation.2 | async-start | bytes 5242880 | tf_op jit(solution)/shard_map/all_to_all | solution.py:61
  43.3 0.1 broadcast_in_dim.28
  43.4 0.1 eq.139
  43.4 0.0 copy-done
  43.4 3.1 %convolution_convert_fusion = bf16[512,2560]{1,0:T(8,128)(2,1)} fusion(bf16[512,2560]{1,0:T(8,128)(2,1)S(1)} %copy-done, s32[512]{0:T(512)S(1)} %multiply_add_fusion), kind=kOutput, calls=%fused_computation.1 | convolution fusion | flops 1343750144 | bytes 5244928 | tf_op jit(solution)/shard_map/dot_general | solution.py:12
  46.5 54.8 %all-to-all-done.1 = bf16[8,64,2560]{2,1,0:T(8,128)(2,1)} async-done(((bf16[8,64,2560]{2,1,0:T(8,128)(2,1)}), bf16[8,64,2560]{2,1,0:T(8,128)(2,1)}, u32[]{:S(2)}, u32[]{:S(2)}) %all-to-all-start.1) | async-done | bytes 2621472 | tf_op jit(solution)/shard_map/all_to_all | solution.py:61
  101.4 4.4 %all-to-all-start.4 = ((bf16[8,64,2560]{2,1,0:T(8,128)(2,1)}), bf16[8,64,2560]{2,1,0:T(8,128)(2,1)}, u32[]{:S(2)}, u32[]{:S(2)}) async-start(bf16[8,64,2560]{2,1,0:T(8,128)(2,1)} %bitcast.42), calls=%async_computation.5 | async-start | bytes 5242880 | tf_op jit(solution)/shard_map/all_to_all | solution.py:61
  105.8 0.0 all-reduce.2.cloned.1.call-start
  105.8 1.5 compare_select_fusion.2
  107.3 0.5 fusion.33
  107.8 3.3 %compare_select_fusion.3 = f32[512,512]{0,1:T(8,128)S(1)} fusion(bf16[512,2560]{1,0:T(8,128)(2,1)} %bitcast.3, bf16[512,2560]{1,0:T(8,128)(2,1)S(1)} %copy-done, s32[512]{0:T(512)S(1)} %eq.139, s32[512]{0:T(512)S(1)} %get-tuple-element.7), kind=kOutput, calls=%fused_computation.7 | convolution fusion | flops 1342701568 | bytes 6295552 | tf_op jit(solution)/shard_map/dot_general | solution.py:12
  111.1 0.5 fusion.34
  111.5 0.6 pad_maximum_fusion
  112.2 0.0 all-reduce.2.cloned.1.call-update
  112.2 0.0 copy-start.1
  112.2 0.0 reduce-scatter.2.cloned.1.call-start
  112.2 5.4 %fusion.69 = f32[512,768]{1,0:T(8,128)} fusion(bf16[512,2560]{1,0:T(8,128)(2,1)S(1)} %copy-done, bf16[2560,768]{1,0:T(8,128)(2,1)} %param.8), kind=kOutput, calls=%fused_computation.110 | convolution fusion | flops 2013265920 | bytes 8126464 | tf_op jit(solution)/shard_map/dot_general | solution.py:12
  117.7 0.0 reduce-scatter.2.cloned.1.call-update
  117.7 0.0 copy-done.1
  117.7 0.1 broadcast_in_dim.57
  117.8 0.1 reshape.166
  117.9 2.2 %convolution_convert_fusion.4 = bf16[512,384]{1,0:T(8,128)(2,1)} fusion(s32[512]{0:T(512)S(1)} %multiply_add_fusion, bf16[512,768]{1,0:T(8,128)(2,1)} %param.13, s32[]{:T(128)S(6)} %select_n.111), kind=kOutput, calls=%fused_computation.15 | convolution fusion | flops 201785344 | bytes 788484 | tf_op jit(solution)/shard_map/dot_general | solution.py:12
  120.1 6.9 %fusion.70 = f32[512,2560]{1,0:T(8,128)} fusion(bf16[512,768]{1,0:T(8,128)(2,1)} %param.13, bf16[2560,768]{1,0:T(8,128)(2,1)} %param.8), kind=kOutput, calls=%fused_computation.111 | convolution fusion | flops 2013265920 | bytes 9961472 | tf_op jit(solution)/shard_map/dot_general | solution.py:12
  127.0 4.3 %all-reduce.2.cloned.1.call-done = f32[512,32]{0,1:T(8,128)} async-done(((f32[512,32]{0,1:T(8,128)}), f32[512,32]{0,1:T(8,128)}) %all-reduce.2.cloned.1.call-update) | async-done | bytes 65552 | tf_op jit(solution)/shard_map/psum | solution.py:83
  131.3 0.8 broadcast_multiply_fusion
  132.2 0.3 convolution_convert_fusion.5
  132.5 0.1 reshape.167
  132.6 0.7 reshape.182
  133.3 31.4 %all-to-all-done.4 = bf16[8,64,2560]{2,1,0:T(8,128)(2,1)} async-done(((bf16[8,64,2560]{2,1,0:T(8,128)(2,1)}), bf16[8,64,2560]{2,1,0:T(8,128)(2,1)}, u32[]{:S(2)}, u32[]{:S(2)}) %all-to-all-start.4) | async-done | bytes 2621472 | tf_op jit(solution)/shard_map/all_to_all | solution.py:61
  164.8 3.6 %all-to-all-start.3 = ((bf16[8,2,1024]{2,1,0:T(2,128)(2,1)}), bf16[8,2,1024]{2,1,0:T(2,128)(2,1)S(1)}, u32[]{:S(2)}, u32[]{:S(2)}) async-start(bf16[8,2,1024]{2,1,0:T(2,128)(2,1)} %reshape.182), calls=%async_computation.4 | async-start | bytes 65536 | tf_op jit(solution)/shard_map/all_to_all | solution.py:61
  168.4 6.7 %all-to-all-done.3 = bf16[8,2,1024]{2,1,0:T(2,128)(2,1)S(1)} async-done(((bf16[8,2,1024]{2,1,0:T(2,128)(2,1)}), bf16[8,2,1024]{2,1,0:T(2,128)(2,1)S(1)}, u32[]{:S(2)}, u32[]{:S(2)}) %all-to-all-start.3) | async-done | bytes 32800 | tf_op jit(solution)/shard_map/all_to_all | solution.py:61
  175.1 3.6 %all-to-all-start.5 = ((bf16[8,64,384]{2,1,0:T(8,128)(2,1)}), bf16[8,64,384]{2,1,0:T(8,128)(2,1)S(1)}, u32[]{:S(2)}, u32[]{:S(2)}) async-start(bf16[8,64,384]{2,1,0:T(8,128)(2,1)} %bitcast.11), calls=%async_computation.6 | async-start | bytes 786432 | tf_op jit(solution)/shard_map/all_to_all | solution.py:61
  178.7 6.6 %add_convert_fusion = bf16[512,2560]{1,0:T(8,128)(2,1)} fusion(f32[512,2560]{1,0:T(8,128)} %fusion.70, bf16[512,2560]{1,0:T(8,128)(2,1)} %bitcast.3, bf16[512,16]{0,1:T(8,128)(2,1)S(1)} %fusion.29, s32[512]{0:T(512)S(1)} %eq.139, s32[512]{0:T(512)S(1)} %get-tuple-element.7, s32[512]{0:T(512)S(1)} %get-tuple-element.6), kind=kOutput, calls=%fused_computation | convolution fusion | flops 1353981952 | bytes 10508288 | tf_op jit(solution)/shard_map/dot_general | solution.py:12
  185.3 0.0 reduce-scatter.2.cloned.1.call-done
  185.3 2.6 %fusion.3 = bf16[512,384]{1,0:T(8,128)(2,1)} fusion(f32[512,384]{1,0:T(8,128)} %reduce-scatter.2.cloned.1.call-done, bf16[512,384]{1,0:T(8,128)(2,1)S(1)} %bitcast.44, s32[512]{0:T(512)S(1)} %eq.139, s32[512]{0:T(512)S(1)} %get-tuple-element.7, s32[512]{0:T(512)S(1)} %get-tuple-element.6, f32[512,32]{0,1:T(8,128)S(1)} %broadcast_multiply_fusion), kind=kOutput, calls=%fused_computation.13 | convolution fusion | flops 211099648 | bytes 1595392 | tf_op jit(solution)/shard_map/dot_general | solution.py:12
  188.0 0.1 reshape.183
  188.1 0.1 reshape.168
  188.2 3.9 %convolution_convert_fusion.2 = bf16[256,2560]{1,0:T(8,128)(2,1)} fusion(bf16[512,2560]{1,0:T(8,128)(2,1)} %bitcast.9, s32[256]{0:T(256)S(1)} %get-tuple-element.9, s32[512]{0:T(512)S(1)} %reshape.159, bf16[512,32]{0,1:T(8,128)(2,1)S(1)} %reshape.168, s32[256]{0:T(256)S(1)} %get-tuple-element.8), kind=kOutput, calls=%fused_computation.3 | convolution fusion | flops 676335616 | bytes 3952640 | tf_op jit(solution)/shard_map/dot_general | solution.py:12
  192.2 0.0 all-to-all-done.5
  192.2 1.3 fusion.6
  (11 shorter events, 0.1 us)
Async XLA Ops:
  7.2 36.3 %copy-start = (bf16[512,2560]{1,0:T(8,128)(2,1)S(1)}, bf16[512,2560]{1,0:T(8,128)(2,1)}, u32[]{:S(2)}) copy-start(bf16[512,2560]{1,0:T(8,128)(2,1)} %param.7) | copy-start | bytes 7864324
  9.0 13.7 %all-to-all-start = ((s32[8,1,4]{2,1,0:T(1,128)}), s32[8,1,4]{2,1,0:T(1,128)S(1)}, u32[]{:S(2)}, u32[]{:S(2)}) async-start(s32[8,1,4]{2,1,0:T(1,128)} %bitcast), calls=%async_computation.1 | async-start | bytes 8192 | tf_op jit(solution)/shard_map/all_to_all | solution.py:38
  24.9 13.9 %all-to-all-start.2 = ((bf16[8,64,384]{2,1,0:T(8,128)(2,1)}), bf16[8,64,384]{2,1,0:T(8,128)(2,1)S(1)}, u32[]{:S(2)}, u32[]{:S(2)}) async-start(bf16[8,64,384]{2,1,0:T(8,128)(2,1)} %bitcast.6), calls=%async_computation.3 | async-start | bytes 786432 | tf_op jit(solution)/shard_map/all_to_all | solution.py:61
  38.9 62.5 %all-to-all-start.1 = ((bf16[8,64,2560]{2,1,0:T(8,128)(2,1)}), bf16[8,64,2560]{2,1,0:T(8,128)(2,1)}, u32[]{:S(2)}, u32[]{:S(2)}) async-start(bf16[8,64,2560]{2,1,0:T(8,128)(2,1)} %bitcast.41), calls=%async_computation.2 | async-start | bytes 5242880 | tf_op jit(solution)/shard_map/all_to_all | solution.py:61
  101.4 63.4 %all-to-all-start.4 = ((bf16[8,64,2560]{2,1,0:T(8,128)(2,1)}), bf16[8,64,2560]{2,1,0:T(8,128)(2,1)}, u32[]{:S(2)}, u32[]{:S(2)}) async-start(bf16[8,64,2560]{2,1,0:T(8,128)(2,1)} %bitcast.42), calls=%async_computation.5 | async-start | bytes 5242880 | tf_op jit(solution)/shard_map/all_to_all | solution.py:61
  105.8 25.5 %all-reduce.2.cloned.1.call-start = ((), (), s32[]{:S(2)}) async-start(), calls=%async_computation.8 | async-start | bytes 131072 | tf_op jit(solution)/shard_map/psum | solution.py:83
  112.2 5.5 %copy-start.1 = (s32[32]{0:T(128)S(1)}, s32[32]{0:T(128)}, u32[]{:S(2)}) copy-start(s32[32]{0:T(128)} %param.12) | copy-start | bytes 388
  112.2 73.1 %reduce-scatter.2.cloned.1.call-start = ((), (), s32[]{:S(2)}) async-start(), calls=%async_computation.7 | async-start | bytes 2359296 | tf_op jit(solution)/shard_map/reduce_scatter | solution.py:74
  164.8 10.3 %all-to-all-start.3 = ((bf16[8,2,1024]{2,1,0:T(2,128)(2,1)}), bf16[8,2,1024]{2,1,0:T(2,128)(2,1)S(1)}, u32[]{:S(2)}, u32[]{:S(2)}) async-start(bf16[8,2,1024]{2,1,0:T(2,128)(2,1)} %reshape.182), calls=%async_computation.4 | async-start | bytes 65536 | tf_op jit(solution)/shard_map/all_to_all | solution.py:61
  175.1 17.1 %all-to-all-start.5 = ((bf16[8,64,384]{2,1,0:T(8,128)(2,1)}), bf16[8,64,384]{2,1,0:T(8,128)(2,1)S(1)}, u32[]{:S(2)}, u32[]{:S(2)}) async-start(bf16[8,64,384]{2,1,0:T(8,128)(2,1)} %bitcast.11), calls=%async_computation.6 | async-start | bytes 786432 | tf_op jit(solution)/shard_map/all_to_all | solution.py:61
Sparse Core Ops, SparseCore 0:
  112.3 18.9 all-reduce.1
  133.6 10.2 reduce-scatter.1

commit v2 on v1

--- a/solution.py
+++ b/solution.py
@@ -1,6 +1,10 @@
+import functools
+
 import jax
 import jax.numpy as jnp
 from jax import lax
+from jax.experimental import pallas as pl
+from jax.experimental.pallas import tpu as pltpu
 from jax.sharding import PartitionSpec as P
 
 adapter_scale = 2.0
@@ -14,7 +18,7 @@
     )
 
 
-def local(tokens, weight, down, up, index, length, cot):
+def local_ops(tokens, weight, down, up, index, length, cot):
     dp = lax.axis_size("dp")
     seg_dev = index.shape[0]
     rows, half_d = tokens.shape
@@ -97,6 +101,295 @@
     grad_up = (adapter_scale * mm(s_ad, cot_got, 0, 0)).astype(BF)
     return output, input_gradient, grad_down, grad_up.reshape(n_own, rank, half_out)
 
+MESH = pl.DeviceIdType.MESH
+
+
+def kernel(
+    dp, per_owner, seg_len, rank, tile,
+    tokens, weight, down, up, cot, dest, placed_row, live, request,
+    output, input_gradient, grad_down, grad_up,
+    tok_send, tok_got, ad_send, ad_got, req_got, both, both_send, both_got,
+    base, base_got, part, part_got, s_full,
+    req_ss, req_rs, ad_ss, ad_rs, tok_ss, tok_rs, both_ss, both_rs, core_ss, core_rs,
+):
+    me = lax.axis_index("dp")
+    core = lax.axis_index("tensor")
+    rows, half_d = tokens.shape
+    n_ad = down.shape[0]
+    half_out = output.shape[1]
+    blk = per_owner * seg_len
+    tiles = half_d // tile
+    column = pl.multiple_of(core * half_out, 128)
+    other = pl.multiple_of((1 - core) * half_out, 128)
+
+    def peer(k):
+        return lax.rem(me + k, dp)
+
+    def cut(p, size=blk):
+        return pl.ds(pl.multiple_of(p * size, size), size)
+
+    def send(src, dst, ss, rs, k, size=blk):
+        p = peer(k)
+        return pltpu.make_async_remote_copy(
+            src_ref=src.at[cut(p, size)], dst_ref=dst.at[cut(me, size)],
+            send_sem=ss.at[k], recv_sem=rs.at[k],
+            device_id={"dp": p}, device_id_type=MESH,
+        )
+
+    def to_core(src, dst, i):
+        return pltpu.make_async_remote_copy(
+            src_ref=src, dst_ref=dst, send_sem=core_ss.at[i], recv_sem=core_rs.at[i],
+            device_id={"tensor": 1 - core}, device_id_type=MESH,
+        )
+
+    barrier = pltpu.get_barrier_semaphore()
+
+    @pl.loop(1, dp)
+    def _(k):
+        pl.semaphore_signal(barrier, 1, device_id={"dp": peer(k)}, device_id_type=MESH)
+
+    pl.semaphore_signal(barrier, 1, device_id={"tensor": 1 - core}, device_id_type=MESH)
+    pl.semaphore_wait(barrier, dp)
+
+    @pl.loop(1, dp)
+    def _(k):
+        send(request, req_got, req_ss, req_rs, k, 8).start()
+
+    req_got[cut(me, 8)] = request[cut(me, 8)]
+
+    def pack(p, lhs, wide, narrow, narrow_cols, dst, drow):
+        @pl.loop(0, tiles)
+        def _(j):
+            c = pl.ds(pl.multiple_of(j * tile, tile), tile)
+            dst[cut(drow), c] = mm(lhs, wide[:, c]).astype(BF)
+
+        dst[cut(drow), half_d:] = mm(lhs, narrow[:, narrow_cols]).astype(BF)
+
+    def place_of(p):
+        i = lax.broadcasted_iota(jnp.int32, (blk, rows), 0) + p * blk
+        return jnp.where(i == dest[...], 1.0, 0.0).astype(BF)
+
+    def pack_tok(k, dst):
+        p = peer(k)
+        pack(p, place_of(p), tokens, cot, pl.ds(column, half_out), dst, p)
+
+    pack_tok(0, tok_got)
+
+    @pl.loop(1, FIRST)
+    def _(i):
+        k = ORDER(i, dp)
+        pack_tok(k, tok_send)
+        send(tok_send, tok_got, tok_ss, tok_rs, k).start()
+
+    @pl.loop(1, dp)
+    def _(k):
+        send(request, req_got, req_ss, req_rs, k, 8).wait()
+
+    def wanted(p, n):
+        i = lax.broadcasted_iota(jnp.int32, (n, dp * 8), 0)
+        j = lax.broadcasted_iota(jnp.int32, (n, dp * 8), 1)
+        if p is None:
+            hit = j == (i // blk) * 8 + (i % blk) // rank
+        else:
+            hit = j == p * 8 + i // rank
+        return mm(jnp.where(hit, 1.0, 0.0).astype(BF), req_got[...].astype(BF))
+
+    def pack_ad(k, dst):
+        p = peer(k)
+        i = lax.broadcasted_iota(jnp.int32, (blk, n_ad), 0)
+        j = lax.broadcasted_iota(jnp.int32, (blk, n_ad), 1)
+        source = wanted(p, blk) * float(rank) + (i % rank).astype(F32)
+        lhs = jnp.where(source == j.astype(F32), 1.0, 0.0).astype(BF)
+        pack(p, lhs, down, up, pl.ds(column, half_out), dst, p)
+
+    @pl.loop(1, dp)
+    def _(i):
+        k = ORDER(i, dp)
+        pack_ad(k, ad_send)
+        send(ad_send, ad_got, ad_ss, ad_rs, k).start()
+
+    pack_ad(0, ad_got)
+
+    @pl.loop(FIRST, dp)
+    def _(i):
+        k = ORDER(i, dp)
+        pack_tok(k, tok_send)
+        send(tok_send, tok_got, tok_ss, tok_rs, k).start()
+
+    base[...] = jnp.zeros_like(base)
+
+    @pl.loop(0, tiles)
+    def _(j):
+        c = pl.ds(pl.multiple_of(j * tile, tile), tile)
+        base[0] += mm(tokens[:, c], weight[c, pl.ds(column, half_out)])
+        base[1] += mm(tokens[:, c], weight[c, pl.ds(other, half_out)])
+
+    swap_base = to_core(base.at[1], base_got, 0)
+    swap_base.start()
+
+    @pl.loop(1, dp)
+    def _(k):
+        send(ad_send, ad_got, ad_ss, ad_rs, k).wait()
+
+    n_rank = ad_got.shape[0]
+    own_block = placed_row[...] == lax.broadcasted_iota(jnp.int32, (rows, n_rank), 1) // rank
+    s_full[...] = jnp.zeros_like(s_full)
+
+    @pl.loop(0, tiles)
+    def _(j):
+        c = pl.ds(pl.multiple_of(j * tile, tile), tile)
+        s_full[...] += mm(tokens[:, c], ad_got[:, c], 1, 1)
+
+    def lane_map(shape, lane_axis, shift):
+        lane = lax.broadcasted_iota(jnp.int32, shape, lane_axis)
+        i = lax.broadcasted_iota(jnp.int32, shape, 1 - lane_axis)
+        return jnp.where(lane == i % rank + shift, 1.0, 0.0)
+
+    def compact(full, shift):
+        return mm(
+            jnp.where(own_block, full, 0.0), lane_map((n_rank, 128), 1, shift),
+            precision=lax.Precision.HIGHEST,
+        )
+
+    t_full = mm(cot[:, pl.ds(column, half_out)], ad_got[:, half_d:], 1, 1)
+    part[...] = compact(s_full[...], 0) + compact(t_full, rank)
+    swap_part = to_core(part, part_got, 1)
+    swap_part.start()
+    swap_part.wait()
+    lanes = lax.broadcasted_iota(jnp.int32, part.shape, 1)
+    factor = jnp.where(lanes < rank, 1.0, adapter_scale) * live[...]
+    both[...] = ((part[...] + part_got[...]) * factor).astype(BF)
+
+    @pl.loop(1, dp)
+    def _(k):
+        p = peer(k)
+        both_send[cut(p)] = mm(place_of(p), both[...]).astype(BF)
+        send(both_send, both_got, both_ss, both_rs, k).start()
+
+    both_got[cut(me)] = mm(place_of(me), both[...]).astype(BF)
+
+    def widen(shift):
+        wide = mm(both[...], lane_map((128, n_rank), 0, shift).astype(BF))
+        return jnp.where(own_block, wide, 0.0).astype(BF)
+
+    shrunk_wide = widen(0)
+    d_wide = widen(rank)
+    swap_base.wait()
+    extra = mm(shrunk_wide, ad_got[:, half_d:])
+    output[...] = (base[0] + base_got[...] + adapter_scale * extra).astype(BF)
+
+    @pl.loop(0, tiles)
+    def _(j):
+        c = pl.ds(pl.multiple_of(j * tile, tile), tile)
+        frozen = mm(cot[...], weight[c, :], 1, 1)
+        input_gradient[:, c] = (frozen + mm(d_wide, ad_got[:, c])).astype(BF)
+
+    @pl.loop(1, dp)
+    def _(k):
+        send(both_send, both_got, both_ss, both_rs, k).wait()
+
+    n_tok = tok_got.shape[0]
+    ad_i = lax.broadcasted_iota(jnp.int32, (n_tok, n_ad), 1) // rank
+    ad_block = wanted(None, n_tok) == ad_i.astype(F32)
+
+    def widen_ad(shift):
+        wide = mm(both_got[...], lane_map((128, n_ad), 0, shift).astype(BF))
+        return jnp.where(ad_block, wide, 0.0).T.astype(BF)
+
+    s_ad = widen_ad(0)
+    d_ad = widen_ad(rank)
+
+    @pl.loop(1, dp)
+    def _(k):
+        send(tok_send, tok_got, tok_ss, tok_rs, k).wait()
+
+    @pl.loop(0, tiles)
+    def _(j):
+        c = pl.ds(pl.multiple_of(j * tile, tile), tile)
+        grad_down[:, c] = mm(d_ad, tok_got[:, c]).astype(BF)
+
+    grad_up[...] = (adapter_scale * mm(s_ad, tok_got[:, half_d:])).astype(BF)
+
+
+FIRST = 3
+
+
+def ORDER(i, dp):
+    return lax.rem(i + dp // 2 - 2, dp - 1) + 1
+
+
+def local(tokens, weight, down, up, index, length, cot):
+    dp = lax.axis_size("dp")
+    seg_dev = index.shape[0]
+    rows, half_d = tokens.shape
+    seg_len = rows // seg_dev
+    n_own, rank, full_out = up.shape
+    half_out = full_out // lax.axis_size("tensor")
+    per_owner = max(1, -(-seg_dev // dp))
+    n_ad = n_own * rank
+    if dp * per_owner != seg_dev or per_owner > 8 or rank != seg_len or n_ad % 128 or n_own > 256:
+        return local_ops(tokens, weight, down, up, index, length, cot)
+    owners = index // n_own
+    local_index = index - owners * n_own
+    pos = jnp.arange(seg_dev, dtype=jnp.int32)
+    earlier = (owners[:, None] == owners[None, :]) & (pos[None, :] < pos[:, None])
+    placed = owners * per_owner + jnp.sum(earlier.astype(jnp.int32), axis=1)
+    slot8 = placed // per_owner * 8 + placed % per_owner
+    hit = slot8[None, :] == jnp.arange(dp * 8, dtype=jnp.int32)[:, None]
+    request = jnp.sum(jnp.where(hit, local_index[None, :] + 1, 0), axis=1) - 1
+    request = jnp.broadcast_to(request.astype(F32)[:, None], (dp * 8, n_ad))
+    row_i = jnp.arange(rows, dtype=jnp.int32)
+    placed_row = jnp.repeat(placed, seg_len)
+    dest = (placed_row * seg_len + row_i % seg_len)[None, :]
+    live = (row_i % seg_len < jnp.repeat(length, seg_len)).astype(F32)[:, None]
+    wide = half_d + half_out
+    tile = 512 if half_d % 512 == 0 else 128
+    vmem = pl.BlockSpec(memory_space=pltpu.VMEM)
+    dma = pltpu.SemaphoreType.DMA((dp,))
+    outs = pl.pallas_call(
+        functools.partial(kernel, dp, per_owner, seg_len, rank, tile),
+        out_shape=[
+            jax.ShapeDtypeStruct((rows, half_out), BF),
+            jax.ShapeDtypeStruct((rows, half_d), BF),
+            jax.ShapeDtypeStruct((n_ad, half_d), BF),
+            jax.ShapeDtypeStruct((n_ad, half_out), BF),
+        ],
+        in_specs=[vmem] * 9,
+        out_specs=[vmem] * 4,
+        scratch_shapes=[
+            pltpu.VMEM((rows, wide), BF),
+            pltpu.VMEM((rows, wide), BF),
+            pltpu.VMEM((rows, wide), BF),
+            pltpu.VMEM((rows, wide), BF),
+            pltpu.VMEM((dp * 8, n_ad), F32),
+            pltpu.VMEM((rows, 128), BF),
+            pltpu.VMEM((rows, 128), BF),
+            pltpu.VMEM((rows, 128), BF),
+            pltpu.VMEM((2, rows, half_out), F32),
+            pltpu.VMEM((rows, half_out), F32),
+            pltpu.VMEM((rows, 128), F32),
+            pltpu.VMEM((rows, 128), F32),
+            pltpu.VMEM((rows, rows), F32),
+            dma, dma, dma, dma, dma, dma, dma, dma,
+            pltpu.SemaphoreType.DMA((2,)),
+            pltpu.SemaphoreType.DMA((2,)),
+        ],
+        compiler_params=pltpu.CompilerParams(
+            collective_id=0, has_side_effects=True, vmem_limit_bytes=56 * 2**20
+        ),
+        cost_estimate=pl.CostEstimate(
+            flops=8 * rows * half_d * full_out, bytes_accessed=16 * rows * half_d, transcendentals=0
+        ),
+    )(
+        tokens, weight, down.reshape(n_ad, half_d), up.reshape(n_ad, full_out),
+        cot, dest, placed_row[:, None], live, request,
+    )
+    output, input_gradient, grad_down, grad_up = outs
+    return (
+        output, input_gradient,
+        grad_down.reshape(n_own, rank, half_d), grad_up.reshape(n_own, rank, half_out),
+    )
+
 
 def solution(mesh):
     in_specs = (

time: 201 us -> 162 us (0.81)
  Pallas kernels: 0 us -> 149 us
  waiting for transfers between devices: 110 us -> 0 us
  matrix products: 43.8 us -> 0 us
  starting transfers between devices: 26.9 us -> 0 us
  between operations: 14.2 us -> 0.67 us
  local copies, waits for them, and re-layouts: 2.35 us -> 9.88 us
    pallas_call x0 -> x1, Pallas kernels: none -> 149 us  [local(): pl.pallas_call(functools.partial(kernel, dp, per_owner, seg_len, rank, ti...]
    all_to_all x6 -> x0, waiting for transfers between devices: 106 us -> none  [the longest x5 99.7 us: exchange(): lax.all_to_all(x.reshape(dp, x.shape[0] // dp, x.shape[1]), 'dp', split_a...]
    dot_general x15 -> x0, matrix products: 43.8 us -> none  [mm(): lax.dot_general(a, b, (((ca,), (cb,)), ((), ())), preferred_element_type=...]
    all_to_all x6 -> x0, starting transfers between devices: 26.8 us -> none  [the longest x5 19.5 us: exchange(): lax.all_to_all(x.reshape(dp, x.shape[0] // dp, x.shape[1]), 'dp', split_a...]
    unnamed x6 -> x8, local copies, waits for them, and re-layouts: 0.85 us -> 7.08 us
    psum x1 -> x0, waiting for transfers between devices: 4.3 us -> none  [local(): sums = lax.psum(parts, 'tensor') * live]
  transfers between devices with their start and end apart: 8 -> 0, of which waited for: 6 -> 0; matrix products, arithmetic and copies ran while one was open for 22% -> 0% of each run, Pallas kernels for 0% -> 0%
where the time goes in v2:
time: 162 us
  Pallas kernels  149 us (92%)
  local copies, waits for them, and re-layouts  9.88 us (6%)
  other arithmetic  2.29 us (1%)
    pallas_call x1, Pallas kernels, local(): pl.pallas_call(functools.partial(kernel, dp, per_owner, seg_len, rank, ti...  149 us
    unnamed x8, local copies, waits for them, and re-layouts  7.08 us

profile of v2, /device:TPU:0, one launch (start us, length us, event | category | flops | bytes accessed | tf_op | source)
XLA Modules:
  0.0 162.0 jit_solution(7790195945707433463)
XLA Ops:
  0.6 0.7 subtract_add_fusion
  1.3 0.2 convert_reduce_fusion
  1.5 0.1 select_reduce_fusion
  1.6 0.1 broadcast_in_dim.21
  1.7 0.1 broadcast_in_dim.20
  1.8 0.1 mul.36
  1.8 0.6 fusion.1.dest
  2.4 0.7 broadcast_in_dim.22
  3.2 0.1 reshape.107
  3.2 0.2 copy.15
  3.4 0.7 broadcast_in_dim.40.request
  4.2 0.7 convert_element_type.21.live
  4.9 0.9 broadcast_in_dim_reshape.4.placed_row
  5.7 149.2 %shard_map.102 = (bf16[512,384]{1,0:T(8,128)(2,1)}, bf16[512,2560]{1,0:T(8,128)(2,1)}, bf16[256,2560]{1,0:T(8,128)(2,1)}, bf16[256,384]{1,0:T(8,128)(2,1)}) custom-call(bf16[512,2560]{1,0:T(8,128)(2,1)} %tokens.1, bf16[2560,768]{1,0:T(8,128)(2,1)} %weight.1, bf16[256,2560]{1,0:T(8,128)(2,1)} %bitcast.6, bf16[256,768]{1,0:T(8,128)(2,1)} %bitcast.7, ...), custom_call_target="tpu_custom_call" | custom-call | flops 8053063680 | bytes 20971520 | tf_op jit(solution)/shard_map/pallas_call | solution.py:349
  154.9 1.8 %copy.21 = bf16[512,384]{1,0:T(8,128)(2,1)} copy(bf16[512,384]{1,0:T(8,128)(2,1)} %get-tuple-element.20) | data formatting | bytes 786432
  156.7 0.0 copy-start
  156.7 3.5 %copy.22 = bf16[512,2560]{1,0:T(8,128)(2,1)} copy(bf16[512,2560]{1,0:T(8,128)(2,1)} %get-tuple-element.21) | data formatting | bytes 5242880
  160.2 0.0 copy-done
  160.2 0.0 copy-start.1
  160.2 1.1 copy.23
  161.3 0.1 copy-done.1
  161.3 0.7 copy.24
  (4 shorter events, 0.0 us)
Async XLA Ops:
  156.7 3.5 %copy-start = (bf16[256,2560]{1,0:T(8,128)(2,1)S(1)}, bf16[256,2560]{1,0:T(8,128)(2,1)}, u32[]{:S(2)}) copy-start(bf16[256,2560]{1,0:T(8,128)(2,1)} %get-tuple-element.10) | copy-start | bytes 3932164
  160.2 1.1 copy-start.1

commit v3 on v2

--- a/solution.py
+++ b/solution.py
@@ -109,11 +109,16 @@
     tokens, weight, down, up, cot, dest, placed_row, live, request,
     output, input_gradient, grad_down, grad_up,
     tok_send, tok_got, ad_send, ad_got, req_got, both, both_send, both_got,
-    base, base_got, part, part_got, s_full,
+    base, base_got, part, part_got, s_full, mirror, req_far,
     req_ss, req_rs, ad_ss, ad_rs, tok_ss, tok_rs, both_ss, both_rs, core_ss, core_rs,
+    mir_ss, mir_rs, far_ss, far_rs, x_ss, x_rs, reqf_ss, reqf_rs,
 ):
     me = lax.axis_index("dp")
     core = lax.axis_index("tensor")
+    group = lax.axis_index("groups")
+    half = dp // 2
+    first = me // half * half
+    opposite = lax.rem(me + half, dp)
     rows, half_d = tokens.shape
     n_ad = down.shape[0]
     half_out = output.shape[1]
@@ -125,6 +130,15 @@
     def peer(k):
         return lax.rem(me + k, dp)
 
+    def near(j):
+        return first + lax.rem(me - first + j, half)
+
+    def far(p):
+        return lax.rem(p + half, dp)
+
+    def step(p):
+        return lax.rem(p - me + dp, dp)
+
     def cut(p, size=blk):
         return pl.ds(pl.multiple_of(p * size, size), size)
 
@@ -142,6 +156,46 @@
             device_id={"tensor": 1 - core}, device_id_type=MESH,
         )
 
+    def to_near(src, dst, from_part, to_part, ss, rs, j, size=blk):
+        return pltpu.make_async_remote_copy(
+            src_ref=src.at[cut(from_part, size)], dst_ref=dst.at[cut(to_part, size)],
+            send_sem=ss.at[j], recv_sem=rs.at[j],
+            device_id={"dp": near(j)}, device_id_type=MESH,
+        )
+
+    def own_ad(j):
+        return to_near(ad_send, ad_got, near(j), me, ad_ss, ad_rs, j)
+
+    def mirror_ad(j):
+        return to_near(ad_send, ad_got, far(near(j)), opposite, far_ss, far_rs, j)
+
+    def far_request(j):
+        return to_near(request, req_far, far(near(j)), me, reqf_ss, reqf_rs, j, 8)
+
+    piece = n_ad // 2 // PIECES
+
+    def piece_rows(c):
+        return pl.ds(pl.multiple_of((group * PIECES + c) * piece, piece), piece)
+
+    def across(c, which):
+        r = piece_rows(c)
+        src = down.at[r] if which == 0 else up.at[r, pl.ds(column, half_out)]
+        cols = pl.ds(0, half_d) if which == 0 else pl.ds(half_d, half_out)
+        return pltpu.make_async_remote_copy(
+            src_ref=src, dst_ref=mirror.at[r, cols],
+            send_sem=mir_ss.at[which, c], recv_sem=mir_rs.at[which, c],
+            device_id={"dp": opposite}, device_id_type=MESH,
+        )
+
+    def share(c):
+        r = piece_rows(c)
+        return pltpu.make_async_remote_copy(
+            src_ref=mirror.at[r], dst_ref=mirror.at[r],
+            send_sem=x_ss.at[c], recv_sem=x_rs.at[c],
+            device_id={"groups": 1 - group}, device_id_type=MESH,
+        )
+
+    req_far[...] = jnp.zeros_like(req_far)
     barrier = pltpu.get_barrier_semaphore()
 
     @pl.loop(1, dp)
@@ -149,15 +203,26 @@
         pl.semaphore_signal(barrier, 1, device_id={"dp": peer(k)}, device_id_type=MESH)
 
     pl.semaphore_signal(barrier, 1, device_id={"tensor": 1 - core}, device_id_type=MESH)
-    pl.semaphore_wait(barrier, dp)
+    pl.semaphore_signal(barrier, 1, device_id={"groups": 1 - group}, device_id_type=MESH)
+    pl.semaphore_wait(barrier, dp + 1)
 
     @pl.loop(1, dp)
     def _(k):
         send(request, req_got, req_ss, req_rs, k, 8).start()
 
+    @pl.loop(1, half)
+    def _(j):
+        far_request(j).start()
+
+    @pl.loop(0, PIECES)
+    def _(c):
+        across(c, 0).start()
+        across(c, 1).start()
+
     req_got[cut(me, 8)] = request[cut(me, 8)]
-
-    def pack(p, lhs, wide, narrow, narrow_cols, dst, drow):
+    req_far[cut(me, 8)] = request[cut(opposite, 8)]
+
+    def pack(lhs, wide, narrow, narrow_cols, dst, drow):
         @pl.loop(0, tiles)
         def _(j):
             c = pl.ds(pl.multiple_of(j * tile, tile), tile)
@@ -171,13 +236,11 @@
 
     def pack_tok(k, dst):
         p = peer(k)
-        pack(p, place_of(p), tokens, cot, pl.ds(column, half_out), dst, p)
-
-    pack_tok(0, tok_got)
-
-    @pl.loop(1, FIRST)
-    def _(i):
-        k = ORDER(i, dp)
+        pack(place_of(p), tokens, cot, pl.ds(column, half_out), dst, p)
+
+    @pl.loop(1, half)
+    def _(j):
+        k = step(near(j))
         pack_tok(k, tok_send)
         send(tok_send, tok_got, tok_ss, tok_rs, k).start()
 
@@ -185,7 +248,11 @@
     def _(k):
         send(request, req_got, req_ss, req_rs, k, 8).wait()
 
-    def wanted(p, n):
+    @pl.loop(1, half)
+    def _(j):
+        far_request(j).wait()
+
+    def wanted(p, n, req_got=req_got):
         i = lax.broadcasted_iota(jnp.int32, (n, dp * 8), 0)
         j = lax.broadcasted_iota(jnp.int32, (n, dp * 8), 1)
         if p is None:
@@ -194,27 +261,37 @@
             hit = j == p * 8 + i // rank
         return mm(jnp.where(hit, 1.0, 0.0).astype(BF), req_got[...].astype(BF))
 
-    def pack_ad(k, dst):
-        p = peer(k)
+    def pack_ad(p, req, wide, narrow, narrow_cols, dst, drow):
         i = lax.broadcasted_iota(jnp.int32, (blk, n_ad), 0)
         j = lax.broadcasted_iota(jnp.int32, (blk, n_ad), 1)
-        source = wanted(p, blk) * float(rank) + (i % rank).astype(F32)
+        source = wanted(p, blk, req) * float(rank) + (i % rank).astype(F32)
         lhs = jnp.where(source == j.astype(F32), 1.0, 0.0).astype(BF)
-        pack(p, lhs, down, up, pl.ds(column, half_out), dst, p)
-
-    @pl.loop(1, dp)
-    def _(i):
-        k = ORDER(i, dp)
-        pack_ad(k, ad_send)
-        send(ad_send, ad_got, ad_ss, ad_rs, k).start()
-
-    pack_ad(0, ad_got)
-
-    @pl.loop(FIRST, dp)
-    def _(i):
-        k = ORDER(i, dp)
-        pack_tok(k, tok_send)
-        send(tok_send, tok_got, tok_ss, tok_rs, k).start()
+        pack(lhs, wide, narrow, narrow_cols, dst, drow)
+
+    def pack_own(p, dst, drow):
+        pack_ad(p, req_got, down, up, pl.ds(column, half_out), dst, drow)
+
+    def pack_mirror(p, dst, drow):
+        pack_ad(p, req_far, mirror, mirror, pl.ds(half_d, half_out), dst, drow)
+
+    @pl.loop(1, half)
+    def _(j):
+        pack_own(near(j), ad_send, near(j))
+        own_ad(j).start()
+
+    def far_tok(j):
+        return send(tok_send, tok_got, tok_ss, tok_rs, step(far(near(j))))
+
+    @pl.loop(0, half)
+    def _(j):
+        pack_tok(step(far(near(j))), tok_send)
+
+    @pl.loop(0, EARLY)
+    def _(j):
+        far_tok(j).start()
+
+    pack_tok(0, tok_got)
+    pack_own(me, ad_got, me)
 
     base[...] = jnp.zeros_like(base)
 
@@ -227,9 +304,34 @@
     swap_base = to_core(base.at[1], base_got, 0)
     swap_base.start()
 
-    @pl.loop(1, dp)
-    def _(k):
-        send(ad_send, ad_got, ad_ss, ad_rs, k).wait()
+    @pl.loop(0, PIECES)
+    def _(c):
+        across(c, 0).wait()
+        across(c, 1).wait()
+        share(c).start()
+
+    @pl.loop(EARLY, half)
+    def _(j):
+        far_tok(j).start()
+
+    @pl.loop(0, PIECES)
+    def _(c):
+        share(c).wait()
+
+    @pl.loop(1, half)
+    def _(j):
+        pack_mirror(near(j), ad_send, far(near(j)))
+        mirror_ad(j).start()
+
+    pack_mirror(me, ad_got, opposite)
+
+    @pl.loop(1, half)
+    def _(j):
+        own_ad(j).wait()
+
+    @pl.loop(1, half)
+    def _(j):
+        mirror_ad(j).wait()
 
     n_rank = ad_got.shape[0]
     own_block = placed_row[...] == lax.broadcasted_iota(jnp.int32, (rows, n_rank), 1) // rank
@@ -311,11 +413,8 @@
     grad_up[...] = (adapter_scale * mm(s_ad, tok_got[:, half_d:])).astype(BF)
 
 
-FIRST = 3
-
-
-def ORDER(i, dp):
-    return lax.rem(i + dp // 2 - 2, dp - 1) + 1
+PIECES = 4
+EARLY = 1
 
 
 def local(tokens, weight, down, up, index, length, cot):
@@ -327,7 +426,7 @@
     half_out = full_out // lax.axis_size("tensor")
     per_owner = max(1, -(-seg_dev // dp))
     n_ad = n_own * rank
-    if dp * per_owner != seg_dev or per_owner > 8 or rank != seg_len or n_ad % 128 or n_own > 256:
+    if dp * per_owner != seg_dev or per_owner > 8 or rank != seg_len or n_ad % 128 or n_own > 256 or n_ad % (32 * PIECES) or dp % 2 or lax.axis_size("groups") != 2:
         return local_ops(tokens, weight, down, up, index, length, cot)
     owners = index // n_own
     local_index = index - owners * n_own
@@ -370,9 +469,17 @@
             pltpu.VMEM((rows, 128), F32),
             pltpu.VMEM((rows, 128), F32),
             pltpu.VMEM((rows, rows), F32),
+            pltpu.VMEM((n_ad, wide), BF),
+            pltpu.VMEM((dp * 8, n_ad), F32),
             dma, dma, dma, dma, dma, dma, dma, dma,
             pltpu.SemaphoreType.DMA((2,)),
             pltpu.SemaphoreType.DMA((2,)),
+            pltpu.SemaphoreType.DMA((2, PIECES)),
+            pltpu.SemaphoreType.DMA((2, PIECES)),
+            dma, dma,
+            pltpu.SemaphoreType.DMA((PIECES,)),
+            pltpu.SemaphoreType.DMA((PIECES,)),
+            dma, dma,
         ],
         compiler_params=pltpu.CompilerParams(
             collective_id=0, has_side_effects=True, vmem_limit_bytes=56 * 2**20

time: 162 us -> 146 us (0.901)
  Pallas kernels: 149 us -> 132 us
    pallas_call x1, Pallas kernels: 149 us -> 132 us  [local(): pl.pallas_call(functools.partial(kernel, dp, per_owner, seg_len, rank, ti...]
where the time goes in v3:
time: 146 us; the launch traced here: 145 us
  Pallas kernels  132 us (90%)
  local copies, waits for them, and re-layouts  9.88 us (7%)
  other arithmetic  2.29 us (2%)
    pallas_call x1, Pallas kernels, local(): pl.pallas_call(functools.partial(kernel, dp, per_owner, seg_len, rank, ti...  132 us
    unnamed x8, local copies, waits for them, and re-layouts  7.08 us

profile of v3, /device:TPU:0, one launch (start us, length us, event | category | flops | bytes accessed | tf_op | source)
XLA Modules:
  0.0 145.1 jit_solution(1269381802253076174)
XLA Ops:
  0.6 0.7 subtract_add_fusion
  1.3 0.2 convert_reduce_fusion
  1.5 0.1 select_reduce_fusion
  1.6 0.1 broadcast_in_dim.21
  1.7 0.1 broadcast_in_dim.20
  1.8 0.1 mul.36
  1.8 0.6 fusion.1.dest
  2.4 0.7 broadcast_in_dim.22
  3.2 0.1 reshape.107
  3.2 0.2 copy.15
  3.4 0.7 broadcast_in_dim.40.request
  4.2 0.7 convert_element_type.21.live
  4.9 0.9 broadcast_in_dim_reshape.4.placed_row
  5.7 132.3 %shard_map.102 = (bf16[512,384]{1,0:T(8,128)(2,1)}, bf16[512,2560]{1,0:T(8,128)(2,1)}, bf16[256,2560]{1,0:T(8,128)(2,1)}, bf16[256,384]{1,0:T(8,128)(2,1)}) custom-call(bf16[512,2560]{1,0:T(8,128)(2,1)} %tokens.1, bf16[2560,768]{1,0:T(8,128)(2,1)} %weight.1, bf16[256,2560]{1,0:T(8,128)(2,1)} %bitcast.6, bf16[256,768]{1,0:T(8,128)(2,1)} %bitcast.7, ...), custom_call_target="tpu_custom_call" | custom-call | flops 8053063680 | bytes 20971520 | tf_op jit(solution)/shard_map/pallas_call | solution.py:448
  138.1 1.8 %copy.21 = bf16[512,384]{1,0:T(8,128)(2,1)} copy(bf16[512,384]{1,0:T(8,128)(2,1)} %get-tuple-element.20) | data formatting | bytes 786432
  139.8 0.0 copy-start
  139.8 3.5 %copy.22 = bf16[512,2560]{1,0:T(8,128)(2,1)} copy(bf16[512,2560]{1,0:T(8,128)(2,1)} %get-tuple-element.21) | data formatting | bytes 5242880
  143.3 0.0 copy-done
  143.3 0.0 copy-start.1
  143.3 1.1 copy.23
  144.4 0.1 copy-done.1
  144.5 0.7 copy.24
  (4 shorter events, 0.0 us)
Async XLA Ops:
  139.8 3.5 %copy-start = (bf16[256,2560]{1,0:T(8,128)(2,1)S(1)}, bf16[256,2560]{1,0:T(8,128)(2,1)}, u32[]{:S(2)}) copy-start(bf16[256,2560]{1,0:T(8,128)(2,1)} %get-tuple-element.10) | copy-start | bytes 3932164
  143.3 1.1 copy-start.1

commit v4 on v3

--- a/solution.py
+++ b/solution.py
@@ -109,7 +109,7 @@
     tokens, weight, down, up, cot, dest, placed_row, live, request,
     output, input_gradient, grad_down, grad_up,
     tok_send, tok_got, ad_send, ad_got, req_got, both, both_send, both_got,
-    base, base_got, part, part_got, s_full, mirror, req_far,
+    base, base_got, part, part_got, s_full, mirror, req_far, frozen,
     req_ss, req_rs, ad_ss, ad_rs, tok_ss, tok_rs, both_ss, both_rs, core_ss, core_rs,
     mir_ss, mir_rs, far_ss, far_rs, x_ss, x_rs, reqf_ss, reqf_rs,
 ):
@@ -238,12 +238,6 @@
         p = peer(k)
         pack(place_of(p), tokens, cot, pl.ds(column, half_out), dst, p)
 
-    @pl.loop(1, half)
-    def _(j):
-        k = step(near(j))
-        pack_tok(k, tok_send)
-        send(tok_send, tok_got, tok_ss, tok_rs, k).start()
-
     @pl.loop(1, dp)
     def _(k):
         send(request, req_got, req_ss, req_rs, k, 8).wait()
@@ -282,13 +276,26 @@
     def far_tok(j):
         return send(tok_send, tok_got, tok_ss, tok_rs, step(far(near(j))))
 
-    @pl.loop(0, half)
+    def near_toks(when):
+        if when == NEAR:
+            @pl.loop(1, half)
+            def _(j):
+                send(tok_send, tok_got, tok_ss, tok_rs, step(near(j))).start()
+
+    @pl.loop(0, EARLY)
     def _(j):
         pack_tok(step(far(near(j))), tok_send)
-
-    @pl.loop(0, EARLY)
-    def _(j):
         far_tok(j).start()
+
+    @pl.loop(EARLY, half)
+    def _(j):
+        pack_tok(step(far(near(j))), tok_send)
+
+    @pl.loop(1, half)
+    def _(j):
+        pack_tok(step(near(j)), tok_send)
+
+    near_toks(0)
 
     pack_tok(0, tok_got)
     pack_own(me, ad_got, me)
@@ -303,6 +310,11 @@
 
     swap_base = to_core(base.at[1], base_got, 0)
     swap_base.start()
+
+    @pl.loop(0, tiles)
+    def _(j):
+        c = pl.ds(pl.multiple_of(j * tile, tile), tile)
+        frozen[:, c] = mm(cot[...], weight[c, :], 1, 1)
 
     @pl.loop(0, PIECES)
     def _(c):
@@ -310,9 +322,11 @@
         across(c, 1).wait()
         share(c).start()
 
-    @pl.loop(EARLY, half)
+    @pl.loop(EARLY, MIDDLE)
     def _(j):
         far_tok(j).start()
+
+    near_toks(1)
 
     @pl.loop(0, PIECES)
     def _(c):
@@ -329,19 +343,37 @@
     def _(j):
         own_ad(j).wait()
 
-    @pl.loop(1, half)
-    def _(j):
-        mirror_ad(j).wait()
+    s_full[...] = jnp.zeros_like(s_full)
+
+    def scores(from_part):
+        r = pl.ds(pl.multiple_of(from_part * blk, half * blk), half * blk)
+
+        @pl.loop(0, tiles)
+        def _(j):
+            c = pl.ds(pl.multiple_of(j * tile, tile), tile)
+            s_full[:, r] += mm(tokens[:, c], ad_got[r, c], 1, 1)
+
+    scores(first)
+
+    @pl.loop(1, half)
+    def _(j):
+        mirror_ad(j).wait_send()
+
+    near_toks(2)
+
+    @pl.loop(MIDDLE, half)
+    def _(j):
+        far_tok(j).start()
+
+    @pl.loop(1, half)
+    def _(j):
+        mirror_ad(j).wait_recv()
+
+    near_toks(3)
+    scores(half - first)
 
     n_rank = ad_got.shape[0]
     own_block = placed_row[...] == lax.broadcasted_iota(jnp.int32, (rows, n_rank), 1) // rank
-    s_full[...] = jnp.zeros_like(s_full)
-
-    @pl.loop(0, tiles)
-    def _(j):
-        c = pl.ds(pl.multiple_of(j * tile, tile), tile)
-        s_full[...] += mm(tokens[:, c], ad_got[:, c], 1, 1)
-
     def lane_map(shape, lane_axis, shift):
         lane = lax.broadcasted_iota(jnp.int32, shape, lane_axis)
         i = lax.broadcasted_iota(jnp.int32, shape, 1 - lane_axis)
@@ -383,8 +415,7 @@
     @pl.loop(0, tiles)
     def _(j):
         c = pl.ds(pl.multiple_of(j * tile, tile), tile)
-        frozen = mm(cot[...], weight[c, :], 1, 1)
-        input_gradient[:, c] = (frozen + mm(d_wide, ad_got[:, c])).astype(BF)
+        input_gradient[:, c] = (frozen[:, c] + mm(d_wide, ad_got[:, c])).astype(BF)
 
     @pl.loop(1, dp)
     def _(k):
@@ -415,6 +446,8 @@
 
 PIECES = 4
 EARLY = 1
+MIDDLE = 2
+NEAR = 2
 
 
 def local(tokens, weight, down, up, index, length, cot):
@@ -426,7 +459,7 @@
     half_out = full_out // lax.axis_size("tensor")
     per_owner = max(1, -(-seg_dev // dp))
     n_ad = n_own * rank
-    if dp * per_owner != seg_dev or per_owner > 8 or rank != seg_len or n_ad % 128 or n_own > 256 or n_ad % (32 * PIECES) or dp % 2 or lax.axis_size("groups") != 2:
+    if dp * per_owner != seg_dev or per_owner > 8 or rank != seg_len or n_ad % 128 or n_own > 256 or n_ad % (32 * PIECES) or dp % 2 or (dp // 2 * per_owner * seg_len) % 128 or lax.axis_size("groups") != 2:
         return local_ops(tokens, weight, down, up, index, length, cot)
     owners = index // n_own
     local_index = index - owners * n_own
@@ -471,6 +504,7 @@
             pltpu.VMEM((rows, rows), F32),
             pltpu.VMEM((n_ad, wide), BF),
             pltpu.VMEM((dp * 8, n_ad), F32),
+            pltpu.VMEM((rows, half_d), F32),
             dma, dma, dma, dma, dma, dma, dma, dma,
             pltpu.SemaphoreType.DMA((2,)),
             pltpu.SemaphoreType.DMA((2,)),

time: 146 us -> 138 us (0.945)
  Pallas kernels: 132 us -> 125 us
    pallas_call x1, Pallas kernels: 132 us -> 125 us  [local(): pl.pallas_call(functools.partial(kernel, dp, per_owner, seg_len, rank, ti...]
where the time goes in v4:
time: 138 us; the launch traced here: 137 us
  Pallas kernels  125 us (91%)
  local copies, waits for them, and re-layouts  9.88 us (7%)
  other arithmetic  2.29 us (2%)
    pallas_call x1, Pallas kernels, local(): pl.pallas_call(functools.partial(kernel, dp, per_owner, seg_len, rank, ti...  125 us
    unnamed x8, local copies, waits for them, and re-layouts  7.08 us

profile of v4, /device:TPU:0, one launch (start us, length us, event | category | flops | bytes accessed | tf_op | source)
XLA Modules:
  0.0 137.4 jit_solution(17148760997487104556)
XLA Ops:
  0.6 0.7 subtract_add_fusion
  1.3 0.2 convert_reduce_fusion
  1.5 0.1 select_reduce_fusion
  1.6 0.1 broadcast_in_dim.21
  1.7 0.1 broadcast_in_dim.20
  1.8 0.1 mul.36
  1.8 0.6 fusion.1.dest
  2.4 0.7 broadcast_in_dim.22
  3.2 0.1 reshape.107
  3.2 0.2 copy.15
  3.4 0.7 broadcast_in_dim.40.request
  4.2 0.7 convert_element_type.21.live
  4.9 0.9 broadcast_in_dim_reshape.4.placed_row
  5.7 124.5 %shard_map.102 = (bf16[512,384]{1,0:T(8,128)(2,1)}, bf16[512,2560]{1,0:T(8,128)(2,1)}, bf16[256,2560]{1,0:T(8,128)(2,1)}, bf16[256,384]{1,0:T(8,128)(2,1)}) custom-call(bf16[512,2560]{1,0:T(8,128)(2,1)} %tokens.1, bf16[2560,768]{1,0:T(8,128)(2,1)} %weight.1, bf16[256,2560]{1,0:T(8,128)(2,1)} %bitcast.6, bf16[256,768]{1,0:T(8,128)(2,1)} %bitcast.7, ...), custom_call_target="tpu_custom_call" | custom-call | flops 8053063680 | bytes 20971520 | tf_op jit(solution)/shard_map/pallas_call | solution.py:481
  130.3 1.8 %copy.21 = bf16[512,384]{1,0:T(8,128)(2,1)} copy(bf16[512,384]{1,0:T(8,128)(2,1)} %get-tuple-element.20) | data formatting | bytes 786432
  132.1 0.0 copy-start
  132.1 3.5 %copy.22 = bf16[512,2560]{1,0:T(8,128)(2,1)} copy(bf16[512,2560]{1,0:T(8,128)(2,1)} %get-tuple-element.21) | data formatting | bytes 5242880
  135.6 0.0 copy-done
  135.6 0.0 copy-start.1
  135.6 1.1 copy.23
  136.6 0.1 copy-done.1
  136.7 0.7 copy.24
  (4 shorter events, 0.0 us)
Async XLA Ops:
  132.1 3.5 %copy-start = (bf16[256,2560]{1,0:T(8,128)(2,1)S(1)}, bf16[256,2560]{1,0:T(8,128)(2,1)}, u32[]{:S(2)}) copy-start(bf16[256,2560]{1,0:T(8,128)(2,1)} %get-tuple-element.10) | copy-start | bytes 3932164
  135.6 1.1 copy-start.1

commit v5 on v4

--- a/solution.py
+++ b/solution.py
@@ -444,7 +444,7 @@
     grad_up[...] = (adapter_scale * mm(s_ad, tok_got[:, half_d:])).astype(BF)
 
 
-PIECES = 4
+PIECES = 8
 EARLY = 1
 MIDDLE = 2
 NEAR = 2

time: 138 us -> 137 us (level)
  no operation moved by 1% of the time
where the time goes in v5:
time: 137 us
  Pallas kernels  124 us (91%)
  local copies, waits for them, and re-layouts  9.88 us (7%)
  other arithmetic  2.29 us (2%)
    pallas_call x1, Pallas kernels, local(): pl.pallas_call(functools.partial(kernel, dp, per_owner, seg_len, rank, ti...  124 us
    unnamed x8, local copies, waits for them, and re-layouts  7.08 us

profile of v5, /device:TPU:0, one launch (start us, length us, event | category | flops | bytes accessed | tf_op | source)
XLA Modules:
  0.0 137.0 jit_solution(17756970378215701326)
XLA Ops:
  0.6 0.7 subtract_add_fusion
  1.3 0.2 convert_reduce_fusion
  1.5 0.1 select_reduce_fusion
  1.6 0.1 broadcast_in_dim.21
  1.7 0.1 broadcast_in_dim.20
  1.8 0.1 mul.36
  1.8 0.6 fusion.1.dest
  2.4 0.7 broadcast_in_dim.22
  3.2 0.1 reshape.107
  3.2 0.2 copy.15
  3.4 0.7 broadcast_in_dim.40.request
  4.2 0.7 convert_element_type.21.live
  4.9 0.9 broadcast_in_dim_reshape.4.placed_row
  5.7 124.1 %shard_map.102 = (bf16[512,384]{1,0:T(8,128)(2,1)}, bf16[512,2560]{1,0:T(8,128)(2,1)}, bf16[256,2560]{1,0:T(8,128)(2,1)}, bf16[256,384]{1,0:T(8,128)(2,1)}) custom-call(bf16[512,2560]{1,0:T(8,128)(2,1)} %tokens.1, bf16[2560,768]{1,0:T(8,128)(2,1)} %weight.1, bf16[256,2560]{1,0:T(8,128)(2,1)} %bitcast.6, bf16[256,768]{1,0:T(8,128)(2,1)} %bitcast.7, ...), custom_call_target="tpu_custom_call" | custom-call | flops 8053063680 | bytes 20971520 | tf_op jit(solution)/shard_map/pallas_call | solution.py:481
  129.9 1.8 %copy.21 = bf16[512,384]{1,0:T(8,128)(2,1)} copy(bf16[512,384]{1,0:T(8,128)(2,1)} %get-tuple-element.20) | data formatting | bytes 786432
  131.7 0.0 copy-start
  131.7 3.5 %copy.22 = bf16[512,2560]{1,0:T(8,128)(2,1)} copy(bf16[512,2560]{1,0:T(8,128)(2,1)} %get-tuple-element.21) | data formatting | bytes 5242880
  135.2 0.0 copy-done
  135.2 0.0 copy-start.1
  135.2 1.1 copy.23
  136.2 0.1 copy-done.1
  136.3 0.7 copy.24
  (4 shorter events, 0.0 us)
Async XLA Ops:
  131.7 3.5 %copy-start = (bf16[256,2560]{1,0:T(8,128)(2,1)S(1)}, bf16[256,2560]{1,0:T(8,128)(2,1)}, u32[]{:S(2)}) copy-start(bf16[256,2560]{1,0:T(8,128)(2,1)} %get-tuple-element.10) | copy-start | bytes 3932164
  135.2 1.1 copy-start.1
